TPU v7x, 32 devices: a whole 2x2x4 slice. The times are simulated.
32 devices in a mesh: gx: 8 (over z, x), gy: 4 (over y, core).
Axes of the slice: x: 2, y: 2, z: 4, core: 2. Of those that a mesh axis runs over, the one named last changes fastest.
Arguments:
- tokens: int32 [65536], P(('gx', 'gy')), may hold values from 0 to 26
- timesteps: int32 [256], P(('gx', 'gy')), may hold values from 0 to 999
- cotangent: bfloat16 [65536, 512], P(('gx', 'gy')), may hold values from -6 to 6
- char_table: bfloat16 [27, 512], P(None, ('gx', 'gy')), may hold values from -6 to 6
- time_weight: bfloat16 [512, 512], P(('gx', 'gy')), may hold values from -0.25 to 0.25
- ln1_gain: bfloat16 [512], P(('gx', 'gy')), may hold values from 0.5 to 1.5
- ln1_bias: bfloat16 [512], P(('gx', 'gy')), may hold values from -4 to 4
- w_qkv: bfloat16 [512, 1536], P(('gx', 'gy')), may hold values from -0.25 to 0.25
- w_attn_out: bfloat16 [512, 512], P(('gx', 'gy')), may hold values from -2 to 2
- ln2_gain: bfloat16 [512], P(('gx', 'gy')), may hold values from 0.5 to 1.5
- ln2_bias: bfloat16 [512], P(('gx', 'gy')), may hold values from -4 to 4
- w_up: bfloat16 [512, 2048], P(('gx', 'gy')), may hold values from -0.25 to 0.25
- w_down: bfloat16 [2048, 512], P(('gx', 'gy')), may hold values from -0.125 to 0.125
Outputs:
- result: float32 [65536, 512], P(('gx', 'gy'))
- d_input: float32 [65536, 512], P(('gx', 'gy'))
- d_char_table: float32 [27, 512], P(None, ('gx', 'gy'))
- d_time_weight: float32 [512, 512], P(('gx', 'gy'))
- d_ln1_gain: float32 [512], P(('gx', 'gy'))
- d_ln1_bias: float32 [512], P(('gx', 'gy'))
- d_w_qkv: float32 [512, 1536], P(('gx', 'gy'))
- d_w_attn_out: float32 [512, 512], P(('gx', 'gy'))
- d_ln2_gain: float32 [512], P(('gx', 'gy'))
- d_ln2_bias: float32 [512], P(('gx', 'gy'))
- d_w_up: float32 [512, 2048], P(('gx', 'gy'))
- d_w_down: float32 [2048, 512], P(('gx', 'gy'))
All inputs are finite; a program needn't handle non-finite values.
Results may differ from a plain program's by a relative error of at most 0.013.
Values may be sent and summed in bfloat16 or wider, within the bound.
A program may use at most 192 MiB of HBM per device.

v0:
```python
import math

import jax
import jax.numpy as jnp
from jax import lax
from jax.sharding import PartitionSpec as P

HEADS = 8


EPSILON = 1e-05
full_precision = lax.Precision.HIGHEST


def contract_rows(left, right):
    return lax.dot_general(
        left, right, (((0,), (0,)), ((), ())), preferred_element_type=jnp.float32
    )


def times_transposed(left, right):
    return lax.dot_general(
        left, right, (((1,), (1,)), ((), ())), preferred_element_type=jnp.float32
    )


def sinusoid(steps, features):
    half_width = features // 2
    frequency = jnp.exp(-math.log(10000.0) * jnp.arange(half_width, dtype=jnp.float32) / half_width)
    angles = steps.astype(jnp.float32)[:, None] * frequency[None, :]
    return jnp.concatenate([jnp.sin(angles), jnp.cos(angles)], axis=1)


def gelu_exact(values):
    return jax.nn.gelu(values, approximate=False)


def norm_parts(values, gain, offset):
    center = jnp.mean(values, axis=-1, keepdims=True)
    shifted = values - center
    inverse = lax.rsqrt(jnp.mean(shifted * shifted, axis=-1, keepdims=True) + EPSILON)
    normed = shifted * inverse
    return (normed * gain + offset, normed, inverse)


def norm_back(grad_out, normed, inverse, gain):
    scaled = grad_out * gain
    grad_in = inverse * (
        scaled
        - jnp.mean(scaled, axis=-1, keepdims=True)
        - normed * jnp.mean(scaled * normed, axis=-1, keepdims=True)
    )
    return (grad_in, jnp.sum(grad_out * normed, axis=0), jnp.sum(grad_out, axis=0))


def attention_parts(start, gain, offset, qkv_weight, seq_count):
    features = start.shape[1]
    head_size = features // HEADS
    normed_in, normed, inverse = norm_parts(
        start, gain.astype(jnp.float32), offset.astype(jnp.float32)
    )
    normed_low = normed_in.astype(jnp.bfloat16)
    project = jnp.dot(normed_low, qkv_weight, preferred_element_type=jnp.float32).astype(
        jnp.bfloat16
    )
    shaped = project.reshape(seq_count, start.shape[0] // seq_count, 3, HEADS, head_size)
    queries = shaped[:, :, 0]
    keys_part = shaped[:, :, 1]
    values_part = shaped[:, :, 2]
    scale_factor = 1.0 / math.sqrt(head_size)
    scores = (
        jnp.einsum("sqhd,skhd->shqk", queries, keys_part, preferred_element_type=jnp.float32)
        * scale_factor
    )
    return (normed_low, normed, inverse, queries, keys_part, values_part, scores, scale_factor)


def attention_forward(start, gain, offset, qkv_weight, proj_weight, seq_count):
    parts = attention_parts(start, gain, offset, qkv_weight, seq_count)
    values_part = parts[5]
    scores = parts[6]
    highest = jnp.max(scores, axis=-1, keepdims=True)
    exponent = jnp.exp(scores - highest)
    totals = jnp.sum(exponent, axis=-1, keepdims=True)
    probabilities = exponent / totals
    mixed = jnp.einsum(
        "shqk,skhd->sqhd",
        probabilities.astype(jnp.bfloat16),
        values_part,
        preferred_element_type=jnp.float32,
    )
    mixed = mixed.astype(jnp.bfloat16).reshape(start.shape)
    branch = jnp.dot(mixed, proj_weight, preferred_element_type=jnp.float32)
    return (branch, highest + jnp.log(totals))


def attention_backward(
    start, grad_mid, gain, offset, qkv_weight, proj_weight, log_totals, seq_count
):
    normed_low, normed, inverse, queries, keys_part, values_part, scores, scale_factor = (
        attention_parts(start, gain, offset, qkv_weight, seq_count)
    )
    probabilities = jnp.exp(scores - log_totals)
    prob_low = probabilities.astype(jnp.bfloat16)
    mixed = jnp.einsum("shqk,skhd->sqhd", prob_low, values_part, preferred_element_type=jnp.float32)
    mixed = mixed.astype(jnp.bfloat16).reshape(start.shape)
    grad_branch = grad_mid.astype(jnp.bfloat16)
    grad_proj = contract_rows(mixed, grad_branch)
    grad_mixed = (
        times_transposed(grad_branch, proj_weight).astype(jnp.bfloat16).reshape(queries.shape)
    )
    grad_values = jnp.einsum(
        "shqk,sqhd->skhd", prob_low, grad_mixed, preferred_element_type=jnp.float32
    )
    grad_probs = jnp.einsum(
        "sqhd,skhd->shqk", grad_mixed, values_part, preferred_element_type=jnp.float32
    )
    grad_scores = (
        probabilities * (grad_probs - jnp.sum(grad_probs * probabilities, axis=-1, keepdims=True))
    ).astype(jnp.bfloat16)
    grad_queries = (
        jnp.einsum("shqk,skhd->sqhd", grad_scores, keys_part, preferred_element_type=jnp.float32)
        * scale_factor
    )
    grad_keys = (
        jnp.einsum("shqk,sqhd->skhd", grad_scores, queries, preferred_element_type=jnp.float32)
        * scale_factor
    )
    grad_project = jnp.stack([grad_queries, grad_keys, grad_values], axis=2).astype(jnp.bfloat16)
    grad_project = grad_project.reshape(start.shape[0], 3 * start.shape[1])
    grad_qkv = contract_rows(normed_low, grad_project)
    grad_in, grad_gain, grad_offset = norm_back(
        times_transposed(grad_project, qkv_weight), normed, inverse, gain.astype(jnp.float32)
    )
    return (grad_mid + grad_in, (grad_gain, grad_offset, grad_qkv, grad_proj))


def ffn_parts(middle, gain, offset, up_weight):
    normed_in, normed, inverse = norm_parts(
        middle, gain.astype(jnp.float32), offset.astype(jnp.float32)
    )
    normed_low = normed_in.astype(jnp.bfloat16)
    hidden = jnp.dot(normed_low, up_weight, preferred_element_type=jnp.float32)
    return (normed_low, normed, inverse, hidden)


def ffn_forward(middle, gain, offset, up_weight, down_weight):
    hidden = ffn_parts(middle, gain, offset, up_weight)[3]
    return jnp.dot(
        gelu_exact(hidden).astype(jnp.bfloat16), down_weight, preferred_element_type=jnp.float32
    )


def ffn_backward(middle, grad_out, gain, offset, up_weight, down_weight):
    normed_low, normed, inverse, hidden = ffn_parts(middle, gain, offset, up_weight)
    active, gelu_pull = jax.vjp(gelu_exact, hidden)
    active_low = active.astype(jnp.bfloat16)
    grad_branch = grad_out.astype(jnp.bfloat16)
    grad_down = contract_rows(active_low, grad_branch)
    grad_active = (
        times_transposed(grad_branch, down_weight).astype(jnp.bfloat16).astype(jnp.float32)
    )
    grad_hidden = gelu_pull(grad_active)[0].astype(jnp.bfloat16)
    grad_up = contract_rows(normed_low, grad_hidden)
    grad_in, grad_gain, grad_offset = norm_back(
        times_transposed(grad_hidden, up_weight), normed, inverse, gain.astype(jnp.float32)
    )
    return (grad_out + grad_in, (grad_gain, grad_offset, grad_up, grad_down))


def body(
    tokens,
    timesteps,
    cotangent,
    char_table,
    time_weight,
    ln1_gain,
    ln1_bias,
    w_qkv,
    w_attn_out,
    ln2_gain,
    ln2_bias,
    w_up,
    w_down,
):
    seq_count = timesteps.shape[0]
    row_count = tokens.shape[0]
    seq_length = row_count // seq_count
    char_full, time_full, gain_one, bias_one, qkv_full, proj_full = (
        lax.all_gather(char_table, ("gx", "gy"), axis=1, tiled=True),
        lax.all_gather(time_weight, ("gx", "gy"), axis=0, tiled=True),
        lax.all_gather(ln1_gain, ("gx", "gy"), axis=0, tiled=True),
        lax.all_gather(ln1_bias, ("gx", "gy"), axis=0, tiled=True),
        lax.all_gather(w_qkv, ("gx", "gy"), axis=0, tiled=True),
        lax.all_gather(w_attn_out, ("gx", "gy"), axis=0, tiled=True),
    )
    alphabet = char_full.shape[0]
    features = char_full.shape[1]
    one_hot = tokens[:, None] == jnp.arange(alphabet, dtype=jnp.int32)[None, :]
    chars = jnp.dot(one_hot.astype(jnp.bfloat16), char_full, preferred_element_type=jnp.float32)
    waves = sinusoid(timesteps, features).astype(jnp.bfloat16)
    stamps = jnp.dot(waves, time_full, preferred_element_type=jnp.float32)
    start = (chars.reshape(seq_count, seq_length, features) + stamps[:, None, :]).reshape(
        row_count, features
    )
    attn_branch, log_totals = attention_forward(
        start, gain_one, bias_one, qkv_full, proj_full, seq_count
    )
    middle = start + attn_branch
    gain_two, bias_two, up_full, down_full = (
        lax.all_gather(ln2_gain, ("gx", "gy"), axis=0, tiled=True),
        lax.all_gather(ln2_bias, ("gx", "gy"), axis=0, tiled=True),
        lax.all_gather(w_up, ("gx", "gy"), axis=0, tiled=True),
        lax.all_gather(w_down, ("gx", "gy"), axis=0, tiled=True),
    )
    result = middle + ffn_forward(middle, gain_two, bias_two, up_full, down_full)
    grad_out = cotangent.astype(jnp.float32)
    gain_two, bias_two, up_full, down_full = (
        lax.all_gather(ln2_gain, ("gx", "gy"), axis=0, tiled=True),
        lax.all_gather(ln2_bias, ("gx", "gy"), axis=0, tiled=True),
        lax.all_gather(w_up, ("gx", "gy"), axis=0, tiled=True),
        lax.all_gather(w_down, ("gx", "gy"), axis=0, tiled=True),
    )
    grad_mid, ffn_grads = ffn_backward(middle, grad_out, gain_two, bias_two, up_full, down_full)
    gain_one, bias_one, qkv_full, proj_full = (
        lax.all_gather(ln1_gain, ("gx", "gy"), axis=0, tiled=True),
        lax.all_gather(ln1_bias, ("gx", "gy"), axis=0, tiled=True),
        lax.all_gather(w_qkv, ("gx", "gy"), axis=0, tiled=True),
        lax.all_gather(w_attn_out, ("gx", "gy"), axis=0, tiled=True),
    )
    grad_start, attn_grads = attention_backward(
        start, grad_mid, gain_one, bias_one, qkv_full, proj_full, log_totals, seq_count
    )
    grad_stamps = jnp.sum(grad_start.reshape(seq_count, seq_length, features), axis=1).astype(
        jnp.bfloat16
    )
    grad_time = contract_rows(waves, grad_stamps)
    grad_char = lax.dot_general(
        one_hot.astype(jnp.float32),
        grad_start,
        (((0,), (0,)), ((), ())),
        precision=full_precision,
        preferred_element_type=jnp.float32,
    )
    all_shards = (
        lax.psum_scatter(grad_char, ("gx", "gy"), scatter_dimension=1, tiled=True),
        lax.psum_scatter(grad_time, ("gx", "gy"), scatter_dimension=0, tiled=True),
        lax.psum_scatter(attn_grads[0], ("gx", "gy"), scatter_dimension=0, tiled=True),
        lax.psum_scatter(attn_grads[1], ("gx", "gy"), scatter_dimension=0, tiled=True),
        lax.psum_scatter(attn_grads[2], ("gx", "gy"), scatter_dimension=0, tiled=True),
        lax.psum_scatter(attn_grads[3], ("gx", "gy"), scatter_dimension=0, tiled=True),
        lax.psum_scatter(ffn_grads[0], ("gx", "gy"), scatter_dimension=0, tiled=True),
        lax.psum_scatter(ffn_grads[1], ("gx", "gy"), scatter_dimension=0, tiled=True),
        lax.psum_scatter(ffn_grads[2], ("gx", "gy"), scatter_dimension=0, tiled=True),
        lax.psum_scatter(ffn_grads[3], ("gx", "gy"), scatter_dimension=0, tiled=True),
    )
    return (result, grad_start) + tuple(all_shards)


def solution(mesh):
    return jax.shard_map(
        body,
        mesh=mesh,
        in_specs=(
            P(("gx", "gy")),
            P(("gx", "gy")),
            P(("gx", "gy"), None),
            P(None, ("gx", "gy")),
            P(("gx", "gy"), None),
            P(("gx", "gy")),
            P(("gx", "gy")),
            P(("gx", "gy"), None),
            P(("gx", "gy"), None),
            P(("gx", "gy")),
            P(("gx", "gy")),
            P(("gx", "gy"), None),
            P(("gx", "gy"), None),
        ),
        out_specs=(
            P(("gx", "gy"), None),
            P(("gx", "gy"), None),
            P(None, ("gx", "gy")),
            P(("gx", "gy"), None),
            P(("gx", "gy")),
            P(("gx", "gy")),
            P(("gx", "gy"), None),
            P(("gx", "gy"), None),
            P(("gx", "gy")),
            P(("gx", "gy")),
            P(("gx", "gy"), None),
            P(("gx", "gy"), None),
        ),
        check_vma=False,
    )
```

profile of v0, /device:TPU:0, one launch (start us, length us, event | category | flops | bytes accessed | tf_op | source)
XLA Modules:
  0.0 1223.6 jit_solution(4898403316664311127)
XLA Ops:
  10.1 45.0 %all_gather.39 = bf16[512,512]{1,0:T(8,128)(2,1)S(1)} all-gather(bf16[16,512]{1,0:T(8,128)(2,1)} %param.17), channel_id=1, replica_groups=mesh['gx'=8,'gy'=4] {'gx','gy'}, dimensions={0}, use_global_device_ids=true | all-gather | bytes 540672 | tf_op jit(solution)/shard_map/all_gather | solution.py:191
  55.1 37.3 %all_gather.38 = bf16[27,512]{0,1:T(8,128)(2,1)S(1)} all-gather(bf16[27,16]{0,1:T(8,128)(2,1)} %param.16), channel_id=1, replica_groups=mesh['gx'=8,'gy'=4] {'gx','gy'}, dimensions={1}, use_global_device_ids=true | all-gather | bytes 28512 | tf_op jit(solution)/shard_map/all_gather | solution.py:190
  102.1 37.1 %all-reduce.9 = (bf16[512]{0:T(512)(128)(2,1)S(1)}, bf16[512]{0:T(512)(128)(2,1)S(1)}, bf16[512]{0:T(512)(128)(2,1)S(1)}, bf16[512]{0:T(512)(128)(2,1)S(1)}) all-reduce(bf16[512]{0:T(512)(128)(2,1)S(1)} %dynamic-update-slice.1, bf16[512]{0:T(512)(128)(2,1)S(1)} %dynamic-update-slice, ...), channel_id=1, replica_groups=mesh['gx'=8,'gy'=4] {'gx','gy'}, use_global_device_ids=true, to_apply=%add.1 | all-reduce | flops 2048 | bytes 8192
  139.2 43.4 %all_gather.43 = bf16[512,512]{1,0:T(8,128)(2,1)S(1)} all-gather(bf16[16,512]{1,0:T(8,128)(2,1)S(1)} %copy-done.28), channel_id=1, replica_groups=mesh['gx'=8,'gy'=4] {'gx','gy'}, dimensions={0}, use_global_device_ids=true | all-gather | bytes 540672 | tf_op jit(solution)/shard_map/all_gather | solution.py:195
  182.6 8.9 convolution_convert_fusion
  191.5 16.3 %reshape.122 = bf16[8,256,3,8,64]{4,3,2,1,0:T(8,128)(2,1)} reshape(bf16[2048,1536]{1,0:T(8,128)(2,1)} %convolution_convert_fusion) | data formatting | bytes 12582912 | tf_op jit(solution)/shard_map/reshape | solution.py:66
  207.8 9.2 fusion.61
  217.0 5.1 copy.75
  226.1 6.3 copy.74
  232.4 9.7 multiply_reduce_fusion.1
  242.1 9.7 fusion.13
  251.9 11.4 convert_bitcast_fusion.2
  271.7 6.3 convert_bitcast_fusion
  282.9 44.2 %multiply_convert_fusion.1 = (bf16[2048,2048]{1,0:T(8,128)(2,1)}, f32[2048,2048]{1,0:T(8,128)}, f32[2048,2048]{1,0:T(8,128)}) fusion(bf16[512,2048]{1,0:T(8,128)(2,1)} %all-gather.6.cloned.1.call-done, f32[2048,512]{1,0:T(8,128)} %copy-done.2, f32[512]{0:T(512)S(1)} %convert_element_type.97, f32[512]{0:T(512)S(1)} %convert_element_type.96, ...), kind=kOutput, calls=%fused_computation.14 | convolution fusion | flops 4572839936 | bytes 48254976 | tf_op jit(solution)/shard_map/dot_general | solution.py:143
  327.0 18.8 %fusion.5 = bf16[2048,2048]{1,0:T(8,128)(2,1)} fusion(f32[2048,2048]{1,0:T(8,128)} %get-tuple-element.31, f32[2048,2048]{1,0:T(8,128)} %get-tuple-element.43, bf16[2048,512]{1,0:T(8,128)(2,1)S(1)} %copy-done.17, bf16[2048,512]{1,0:T(8,128)(2,1)} %all-gather.8.cloned.1.call-done), kind=kOutput, calls=%fused_computation.8 | convolution fusion | flops 4362076160 | bytes 46137344 | tf_op jit(solution)/shard_map/dot_general | solution.py:22
  345.8 10.7 multiply_reduce_fusion.2
  365.4 5.3 copy.57
  370.7 11.9 multiply_reduce_fusion
  382.6 12.4 %multiply_convert_fusion = bf16[8,8,256,256]{2,3,1,0:T(8,128)(2,1)S(1)} fusion(f32[8,8,256,256]{2,3,1,0:T(8,128)} %get-tuple-element.46, f32[8,8,256,256]{2,3,1,0:T(8,128)} %get-tuple-element.40, f32[8,8,256]{2,1,0:T(8,128)S(1)} %get-tuple-element.45, f32[8,8,256]{2,1,0:T(8,128)S(1)} %copy-done.20), kind=kLoop, calls=%fused_computation.11 | loop fusion | flops 20971520 | bytes 42074112 | tf_op jit(solution)/shard_map/convert_element_type | solution.py:120
  399.3 8.8 convert_bitcast_fusion.1
  416.4 7.7 multiply_reduce_fusion.3
  438.2 9.3 fusion.45
  447.6 11.4 fusion.58
  460.6 9.7 fusion.63
  470.4 37.3 %all-reduce.8 = (f32[512]{0:T(512)S(1)}, f32[512]{0:T(512)S(1)}, f32[512]{0:T(512)S(1)}, f32[512]{0:T(512)S(1)}) all-reduce(f32[512]{0:T(512)S(1)} %get-tuple-element.14, f32[512]{0:T(512)S(1)} %get-tuple-element.19, f32[512]{0:T(512)S(1)} %get-tuple-element.12, ...), channel_id=4, replica_groups=mesh['gx'=8,'gy'=4] {'gx','gy'}, use_global_device_ids=true, to_apply=%region_15.0.clone | all-reduce | flops 2048 | bytes 16384
  510.0 10.1 convolution_add_fusion
  520.1 42.0 %reduce-scatter.7.cloned.1.call-done = f32[27,16]{0,1:T(8,128)} async-done(((f32[27,512]{0,1:T(8,128)}), f32[27,16]{0,1:T(8,128)}) %reduce-scatter.7.cloned.1.call-update) | async-done | bytes 1744 | tf_op jit(solution)/shard_map/reduce_scatter | solution.py:246
  562.1 133.5 %reduce-scatter.13.cloned.1.call-done = f32[16,512]{1,0:T(8,128)} async-done(((f32[512,512]{1,0:T(8,128)}), f32[16,512]{1,0:T(8,128)}) %reduce-scatter.13.cloned.1.call-update) | async-done | bytes 32784 | tf_op jit(solution)/shard_map/reduce_scatter | solution.py:251
  695.6 133.4 %reduce-scatter.9.cloned.1.call-done = f32[16,512]{1,0:T(8,128)} async-done(((f32[512,512]{1,0:T(8,128)}), f32[16,512]{1,0:T(8,128)}) %reduce-scatter.9.cloned.1.call-update) | async-done | bytes 32784 | tf_op jit(solution)/shard_map/reduce_scatter | solution.py:247
  828.9 104.4 %reduce-scatter.11.cloned.1.call-done = f32[16,1536]{1,0:T(8,128)} async-done(((f32[512,1536]{1,0:T(8,128)}), f32[16,1536]{1,0:T(8,128)}) %reduce-scatter.11.cloned.1.call-update) | async-done | bytes 98320 | tf_op jit(solution)/shard_map/reduce_scatter | solution.py:250
  933.3 143.1 %reduce-scatter.15.cloned.1.call-done = f32[16,2048]{1,0:T(8,128)} async-done(((f32[512,2048]{1,0:T(8,128)}), f32[16,2048]{1,0:T(8,128)}) %reduce-scatter.15.cloned.1.call-update) | async-done | bytes 131088 | tf_op jit(solution)/shard_map/reduce_scatter | solution.py:254
  1076.4 140.2 %reduce-scatter.17.cloned.1.call-done = f32[64,512]{1,0:T(8,128)} async-done(((f32[2048,512]{1,0:T(8,128)}), f32[64,512]{1,0:T(8,128)}) %reduce-scatter.17.cloned.1.call-update) | async-done | bytes 131088 | tf_op jit(solution)/shard_map/reduce_scatter | solution.py:255
  (156 shorter events, 68.9 us)
Async XLA Ops:
  7.2 175.4 %all-gather.4.cloned.1.call-start = ((), (), s32[]{:S(2)}) async-start(), calls=%async_computation.6 | async-start | bytes 1622016 | tf_op jit(solution)/shard_map/all_gather | solution.py:194
  7.9 275.0 %all-gather.6.cloned.1.call-start = ((), (), s32[]{:S(2)}) async-start(), calls=%async_computation.7 | async-start | bytes 2162688 | tf_op jit(solution)/shard_map/all_gather | solution.py:213
  8.7 318.4 %all-gather.8.cloned.1.call-start = ((), (), s32[]{:S(2)}) async-start(), calls=%async_computation.8 | async-start | bytes 2162688 | tf_op jit(solution)/shard_map/all_gather | solution.py:214
  9.4 552.7 %reduce-scatter.7.cloned.1.call-start = ((), (), s32[]{:S(2)}) async-start(), calls=%async_computation.9 | async-start | bytes 270336 | tf_op jit(solution)/shard_map/reduce_scatter | solution.py:246
  98.7 40.5 %copy-start.28 = (bf16[16,512]{1,0:T(8,128)(2,1)S(1)}, bf16[16,512]{1,0:T(8,128)(2,1)}, u32[]{:S(2)}) copy-start(bf16[16,512]{1,0:T(8,128)(2,1)} %param.21) | copy-start | bytes 49156
  139.2 52.4 %copy-start.29 = (f32[512]{0:T(512)}, f32[512]{0:T(512)S(1)}, u32[]{:S(2)}) copy-start(f32[512]{0:T(512)S(1)} %convert_element_type.89) | copy-start | bytes 6148
  139.2 52.4 %copy-start.31 = (f32[512]{0:T(512)}, f32[512]{0:T(512)S(1)}, u32[]{:S(2)}) copy-start(f32[512]{0:T(512)S(1)} %convert_element_type.90) | copy-start | bytes 6148
  182.6 84.5 %copy-start.14 = (bf16[512,512]{1,0:T(8,128)(2,1)}, bf16[512,512]{1,0:T(8,128)(2,1)S(1)}, u32[]{:S(2)}) copy-start(bf16[512,512]{1,0:T(8,128)(2,1)S(1)} %all_gather.43) | copy-start | bytes 1572868
  226.1 16.0 %copy-start.6 = (bf16[8,256,1,8,64]{1,4,3,0,2:T(8,128)(2,1)}, bf16[8,256,1,8,64]{1,4,3,0,2:T(8,128)(2,1)S(1)}, u32[]{:S(2)}) copy-start(bf16[8,256,1,8,64]{1,4,3,0,2:T(8,128)(2,1)S(1)} %copy.76) | copy-start | bytes 6291460
  242.1 29.5 %slice-start = ((s8[16777216]{0:T(1024)(128)(4,1)}), s8[4194304]{0:T(1024)(128)(4,1)S(1)}, s32[]{:S(2)}) async-start(s8[16777216]{0:T(1024)(128)(4,1)} %bitcast.100), calls=%async_computation.15 | async-start | bytes 8388608
  251.9 19.8 %copy-start.19 = (f32[8,8,256]{2,1,0:T(8,128)}, f32[8,8,256]{2,1,0:T(8,128)S(1)}, u32[]{:S(2)}) copy-start(f32[8,8,256]{2,1,0:T(8,128)S(1)} %log_add_fusion) | copy-start | bytes 196612
  251.9 19.8 %slice-start.1 = ((s8[16777216]{0:T(1024)(128)(4,1)}), s8[4194304]{0:T(1024)(128)(4,1)S(1)}, s32[]{:S(2)}) async-start(s8[16777216]{0:T(1024)(128)(4,1)} %bitcast.100), calls=%async_computation.16 | async-start | bytes 8388608
  251.9 19.8 %slice-start.2 = ((s8[16777216]{0:T(1024)(128)(4,1)}), s8[4194304]{0:T(1024)(128)(4,1)S(1)}, s32[]{:S(2)}) async-start(s8[16777216]{0:T(1024)(128)(4,1)} %bitcast.100), calls=%async_computation.17 | async-start | bytes 8388608
  251.9 19.8 %slice-start.3 = ((s8[16777216]{0:T(1024)(128)(4,1)}), s8[4194304]{0:T(1024)(128)(4,1)S(1)}, s32[]{:S(2)}) async-start(s8[16777216]{0:T(1024)(128)(4,1)} %bitcast.100), calls=%async_computation.18 | async-start | bytes 8388608
  282.9 44.2 %copy-start.17 = (bf16[2048,512]{1,0:T(8,128)(2,1)S(1)}, bf16[2048,512]{1,0:T(8,128)(2,1)}, u32[]{:S(2)}) copy-start(bf16[2048,512]{1,0:T(8,128)(2,1)} %param.15) | copy-start | bytes 6291460
  345.8 10.8 copy-start.3
  365.4 5.3 copy-start.8
  365.4 5.3 copy-start.20
  382.6 12.4 %copy-start.7 = (bf16[8,256,1,8,64]{1,4,3,0,2:T(8,128)(2,1)S(1)}, bf16[8,256,1,8,64]{1,4,3,0,2:T(8,128)(2,1)}, u32[]{:S(2)}) copy-start(bf16[8,256,1,8,64]{1,4,3,0,2:T(8,128)(2,1)} %copy-done.6) | copy-start | bytes 6291460
  416.3 7.7 copy-start.13
  416.4 7.7 copy-start.5
  416.4 7.7 copy-start.22
  425.4 6.6 copy-start.16
  432.0 263.6 %reduce-scatter.13.cloned.1.call-start = ((), (), s32[]{:S(2)}) async-start(), calls=%async_computation.12 | async-start | bytes 1081344 | tf_op jit(solution)/shard_map/reduce_scatter | solution.py:251
  432.1 4.8 copy-start.24
  432.1 4.8 copy-start.26
  432.1 6.1 copy-start.32
  436.6 392.4 %reduce-scatter.9.cloned.1.call-start = ((), (), s32[]{:S(2)}) async-start(), calls=%async_computation.10 | async-start | bytes 1081344 | tf_op jit(solution)/shard_map/reduce_scatter | solution.py:247
  438.2 495.2 %reduce-scatter.11.cloned.1.call-start = ((), (), s32[]{:S(2)}) async-start(), calls=%async_computation.11 | async-start | bytes 3244032 | tf_op jit(solution)/shard_map/reduce_scatter | solution.py:250
  447.5 628.9 %reduce-scatter.15.cloned.1.call-start = ((), (), s32[]{:S(2)}) async-start(), calls=%async_computation.13 | async-start | bytes 4325376 | tf_op jit(solution)/shard_map/reduce_scatter | solution.py:254
  459.0 757.6 %reduce-scatter.17.cloned.1.call-start = ((), (), s32[]{:S(2)}) async-start(), calls=%async_computation.14 | async-start | bytes 4325376 | tf_op jit(solution)/shard_map/reduce_scatter | solution.py:255
  470.3 39.7 %copy-start.33 = (bf16[2048,512]{1,0:T(8,128)(2,1)S(1)}, bf16[2048,512]{1,0:T(8,128)(2,1)}, u32[]{:S(2)}) copy-start(bf16[2048,512]{1,0:T(8,128)(2,1)} %all-gather.8.cloned.1.call-done) | copy-start | bytes 6291460
  (19 other events, 43.9 us)
Sparse Core Ops, SparseCore 0:
  10.9 58.1 all-gather.3
  71.9 55.5 all-gather.5
  130.3 55.9 all-gather.7
  432.1 129.8 reduce-scatter.6
  564.8 130.7 reduce-scatter.12
  698.2 130.6 reduce-scatter.8
  835.8 97.4 reduce-scatter.10
  936.3 140.1 reduce-scatter.14
  1079.4 137.1 reduce-scatter.16
where the time goes:
time: 1230 us; the launch traced here: 1220 us
  waiting for transfers between devices  699 us (57%)
  blocking collectives  200 us (16%)
  matrix products  199 us (16%)
  local copies, waits for them, and re-layouts  79.2 us (6%)
  other arithmetic  30.9 us (3%)
  between operations  14.9 us (1%)
    reduce_scatter x1, waiting for transfers between devices, body(): lax.psum_scatter(ffn_grads[2], ('gx', 'gy'), scatter_dimension=0, tiled=T...  143 us
    reduce_scatter x1, waiting for transfers between devices, body(): lax.psum_scatter(ffn_grads[3], ('gx', 'gy'), scatter_dimension=0, tiled=T...  140 us
    reduce_scatter x1, waiting for transfers between devices, body(): lax.psum_scatter(attn_grads[3], ('gx', 'gy'), scatter_dimension=0, tiled=...  134 us
    reduce_scatter x1, waiting for transfers between devices, body(): lax.psum_scatter(grad_time, ('gx', 'gy'), scatter_dimension=0, tiled=True)  133 us
    reduce_scatter x1, waiting for transfers between devices, body(): lax.psum_scatter(attn_grads[2], ('gx', 'gy'), scatter_dimension=0, tiled=...  104 us
    unnamed x2, blocking collectives  74.4 us
    all_gather x1, blocking collectives, body(): lax.all_gather(time_weight, ('gx', 'gy'), axis=0, tiled=True)  45 us
    dot_general x1, matrix products, ffn_parts(): hidden = jnp.dot(normed_low, up_weight, preferred_element_type=jnp.float32)  44.2 us
  transfers between devices with their start and end apart: 9, of which 6 were waited for; matrix products, arithmetic and copies ran while one was open for 16% of the time, Pallas kernels for 0%

commit v1 on v0

v1 whole, which is shorter than its diff:
```python
import functools
import math

import jax
import jax.numpy as jnp
from jax import lax
from jax.experimental import pallas as pl
from jax.experimental.pallas import tpu as pltpu
from jax.sharding import PartitionSpec as P

F32, BF16 = jnp.float32, jnp.bfloat16

MESH = pl.DeviceIdType.MESH


def place():
    gx, gy = lax.axis_index("gx"), lax.axis_index("gy")
    return gx // 2, gx % 2, gy // 2, gy % 2


def device(z, x, y, c):
    return (z * 2 + x, y * 2 + c)


def greet(nz):
    z, x, y, c = place()
    barrier = pltpu.get_barrier_semaphore()

    def hello(*where):
        pl.semaphore_signal(barrier, inc=1, device_id=device(*where), device_id_type=MESH)

    hello(z, x, y, 1 - c)
    hello(z, 1 - x, y, c)
    hello(z, x, 1 - y, c)

    @pl.when(z > 0)
    def _():
        hello(z - 1, x, y, c)

    @pl.when(z < nz - 1)
    def _():
        hello(z + 1, x, y, c)

    pl.semaphore_wait(barrier, 3 + jnp.minimum(z, 1) + jnp.minimum(nz - 1 - z, 1))


def send(src, dst, sems, slot, where):
    send_sems, recv_sems = sems
    return pltpu.make_async_remote_copy(
        src_ref=src, dst_ref=dst, send_sem=send_sems.at[slot], recv_sem=recv_sems.at[slot],
        device_id=device(*where), device_id_type=MESH)


def middle_of(width):
    return width // 256 * 128


GATHER_SLOTS = lambda nz: 2 * (nz - 1) + 4 + 5


class Gather:
    def __init__(self, nz, out, sems):
        self.nz, self.out, self.sems = nz, out, sems
        self.base = 2 * (nz - 1)

    def own(self, value):
        z, x, y, c = place()
        self.out[z, x, y, c] = value

    def along(self, step, act):
        nz = self.nz
        z, x, y, c = place()
        for way, slot in ((1, 2 * (step - 1)), (-1, 2 * (step - 1) + 1)):
            origin = z - way * (step - 1)
            to = z + way
            can_send = (origin >= 0) & (origin < nz) & (to >= 0) & (to < nz)
            arrives = (z - way * step >= 0) & (z - way * step < nz)
            if act == "start":
                @pl.when(can_send)
                def _():
                    send(self.out.at[origin, x, y, c], self.out.at[origin, x, y, c], self.sems, slot, (to, x, y, c)).start()
            elif act == "recv":
                come = z - way * step

                @pl.when(arrives)
                def _():
                    send(self.out.at[come, x, y, c], self.out.at[come, x, y, c], self.sems, slot, (z - way, x, y, c)).wait_recv()
            else:
                @pl.when(can_send)
                def _():
                    send(self.out.at[origin, x, y, c], self.out.at[origin, x, y, c], self.sems, slot, (to, x, y, c)).wait_send()

    def copy(self, name, comes=False):
        z, x, y, c = place()
        half = middle_of(self.out.shape[-1])
        cuts = {"": slice(None), "lo": pl.ds(0, half), "hi": pl.ds(half, self.out.shape[-1] - half)}
        to, a, b, k, cut, slot = {
            "x": ("x", x, y, c, "", 0), "y": ("y", x, y, c, "", 1),
            "xd": ("x", x, 1 - y, c, "lo", 2), "yd": ("y", 1 - x, y, c, "hi", 3),
            "c0": ("c", x, y, c, "", 4), "c1": ("c", 1 - x, y, c, "", 5), "c2": ("c", x, 1 - y, c, "", 6),
            "c3": ("c", 1 - x, 1 - y, c, "lo", 7), "c4": ("c", 1 - x, 1 - y, c, "hi", 8)}[name]
        if comes:
            a, b, k = (1 - a, b, k) if to == "x" else (a, 1 - b, k) if to == "y" else (a, b, 1 - k)
        where = {"x": (z, 1 - x, y, c), "y": (z, x, 1 - y, c), "c": (z, x, y, 1 - c)}[to]
        ref = self.out.at[pl.ds(0, self.nz), a, b, k]
        if cut:
            ref = ref.at[:, :, cuts[cut]]
        return send(ref, ref, self.sems, self.base + slot, where)

    def start(self, *names):
        for name in names:
            self.copy(name).start()

    def arrive(self, *names):
        for name in names:
            self.copy(name, comes=True).wait_recv()

    def along_z(self):
        self.along(1, "start")
        for step in range(1, self.nz):
            self.along(step, "recv")
            if step < self.nz - 1:
                self.along(step + 1, "start")

    def finish(self):
        for step in range(1, self.nz):
            self.along(step, "sent")
        for name in ("x", "y", "xd", "yd", "c0", "c1", "c2", "c3", "c4"):
            self.copy(name).wait_send()


def gather_kernel(nz, count, *refs):
    ins, outs, sems = refs[:count], refs[count:2 * count], refs[2 * count:]
    groups = [Gather(nz, outs[i], (sems[2 * i], sems[2 * i + 1])) for i in range(count)]
    for group, ref in zip(groups, ins):
        group.own(ref[...])
    greet(nz)
    for i, group in enumerate(groups):
        group.along_z()
        group.start("x", "y", "c0")
        if i > 0:
            before = groups[i - 1]
            before.arrive("x", "y")
            before.start("xd", "yd", "c1", "c2")
        if i > 1:
            before = groups[i - 2]
            before.arrive("xd", "yd")
            before.start("c3", "c4")
    last = groups[-1]
    last.arrive("x", "y")
    last.start("xd", "yd", "c1", "c2")
    for group in groups[-2:]:
        group.arrive("xd", "yd")
        group.start("c3", "c4")
    for group in groups:
        group.arrive("c0", "c1", "c2", "c3", "c4")
        group.finish()


def gather(nz, shards):
    count = len(shards)
    sems = []
    for _ in shards:
        sems += [pltpu.SemaphoreType.DMA((GATHER_SLOTS(nz),)), pltpu.SemaphoreType.DMA((GATHER_SLOTS(nz),))]
    vmem = pl.BlockSpec(memory_space=pltpu.VMEM)
    return pl.pallas_call(
        functools.partial(gather_kernel, nz, count),
        out_shape=[jax.ShapeDtypeStruct((nz, 2, 2, 2) + s.shape, s.dtype) for s in shards],
        in_specs=[vmem] * count, out_specs=[vmem] * count, scratch_shapes=sems,
        compiler_params=pltpu.CompilerParams(collective_id=0, has_side_effects=True, vmem_limit_bytes=60 * 2**20),
        name="gather_weights",
    )(*shards)


SCATTER_SLOTS = lambda nz: 2 * (nz - 1) + 5


class Scatter:
    def __init__(self, nz, mine, own, far, near, line, sems):
        self.nz, self.mine, self.own, self.far, self.near, self.line, self.sems = nz, mine, own, far, near, line, sems
        self.width = mine.shape[-1]
        self.half = middle_of(self.width)
        self.base = 2 * (nz - 1)

    def cuts(self):
        return pl.ds(0, self.half), pl.ds(self.half, self.width - self.half)

    def copy(self, name):
        z, x, y, c = place()
        nz, own, sems, base = self.nz, self.own, self.sems, self.base
        lo, hi = self.cuts()
        all_z = pl.ds(0, nz)
        xp, yp, cp = (z, 1 - x, y, c), (z, x, 1 - y, c), (z, x, y, 1 - c)
        if name == "c":
            return send(self.mine.at[all_z, :, :, 1 - c], own, sems, base, cp)
        if name == "xd":
            return send(own.at[all_z, 1 - x, 1 - y, :, lo], self.far.at[:, :, lo], sems, base + 1, xp)
        if name == "yd":
            return send(own.at[all_z, 1 - x, 1 - y, :, hi], self.far.at[:, :, hi], sems, base + 2, yp)
        if name == "x":
            return send(own.at[all_z, 1 - x, y], self.near.at[0], sems, base + 3, xp)
        return send(own.at[all_z, x, 1 - y], self.near.at[1], sems, base + 4, yp)

    def add(self, a, b, value, cols=None):
        cols = cols if cols is not None else pl.ds(0, self.width)

        def one(k, _):
            spot = (k, a, b, slice(None), cols)
            self.own[spot] = (self.own[spot].astype(jnp.float32) + value(k, cols)).astype(self.own.dtype)
            return 0
        lax.fori_loop(0, self.nz, one, 0)

    def cores(self):
        self.copy("c").start()

    def corner(self):
        z, x, y, c = place()
        self.copy("c").wait()
        for a, b in ((1 - x, 1 - y), (1 - x, y), (x, 1 - y), (x, y)):
            self.add(a, b, lambda k, cols, a=a, b=b: self.mine[k, a, b, c, :, cols].astype(jnp.float32))
            if a is not x and b is not y:
                self.copy("xd").start()
                self.copy("yd").start()

    def sides(self):
        z, x, y, c = place()
        lo, hi = self.cuts()
        self.copy("xd").wait()
        self.add(x, 1 - y, lambda k, cols: self.far[k, :, cols].astype(jnp.float32), lo)
        self.copy("y").start()
        self.copy("yd").wait()
        self.add(1 - x, y, lambda k, cols: self.far[k, :, cols].astype(jnp.float32), hi)
        self.copy("x").start()

    def column(self):
        z, x, y, c = place()
        self.copy("x").wait()
        self.copy("y").wait()
        self.add(x, y, lambda k, cols: self.near[0, k, :, cols].astype(jnp.float32) + self.near[1, k, :, cols].astype(jnp.float32))

    def along(self, step, act):
        nz = self.nz
        z, x, y, c = place()
        far = nz - step
        for way, slot in ((1, 2 * (step - 1)), (-1, 2 * (step - 1) + 1)):
            goes = z + way * far
            can_send = (goes >= 0) & (goes < nz)
            comes = z + way * (far - 1)
            back = z - way
            arrives = (back >= 0) & (back < nz) & (comes >= 0) & (comes < nz)
            landing = self.line.at[slot]
            if act == "start":
                @pl.when(can_send)
                def _():
                    send(self.own.at[goes, x, y], landing, self.sems, slot, (z + way, x, y, c)).start()
            elif act == "recv":
                @pl.when(arrives)
                def _():
                    send(self.own.at[comes, x, y], landing, self.sems, slot, (back, x, y, c)).wait_recv()
                    spot = (comes, x, y)
                    self.own[spot] = (self.own[spot].astype(jnp.float32) + self.line[slot].astype(jnp.float32)).astype(self.own.dtype)
            else:
                @pl.when(can_send)
                def _():
                    send(self.own.at[goes, x, y], landing, self.sems, slot, (z + way, x, y, c)).wait_send()

    def total(self):
        z, x, y, c = place()
        for step in range(1, self.nz):
            self.along(step, "sent")
        return self.own[z, x, y].astype(jnp.float32)


def scatter_kernel(nz, count, *refs):
    ins, outs = refs[:count], refs[count:2 * count]
    rest = refs[2 * count:]
    groups = [Scatter(nz, ins[i], *rest[6 * i:6 * i + 4], rest[6 * i + 4:6 * i + 6]) for i in range(count)]
    greet(nz)
    for group in groups:
        group.cores()
    for i in range(count + 3):
        for stage, act in ((3, "line"), (2, "column"), (1, "sides"), (0, "corner")):
            k = i - stage
            if 0 <= k < count:
                if act == "corner":
                    groups[k].corner()
                elif act == "sides":
                    groups[k].sides()
                elif act == "column":
                    groups[k].column()
                    groups[k].along(1, "start")
                else:
                    for step in range(1, nz):
                        groups[k].along(step, "recv")
                        if step < nz - 1:
                            groups[k].along(step + 1, "start")
    for group, out in zip(groups, outs):
        out[...] = group.total()


def scatter_scratch(nz, tail, dtype):
    return [
        pltpu.VMEM((nz, 2, 2) + tail, dtype), pltpu.VMEM((nz,) + tail, dtype), pltpu.VMEM((2, nz) + tail, dtype),
        pltpu.VMEM((2 * (nz - 1),) + tail, dtype),
        pltpu.SemaphoreType.DMA((SCATTER_SLOTS(nz),)), pltpu.SemaphoreType.DMA((SCATTER_SLOTS(nz),))]


def scatter(nz, partials):
    count = len(partials)
    scratch = []
    for p in partials:
        scratch += scatter_scratch(nz, p.shape[4:], p.dtype)
    vmem = pl.BlockSpec(memory_space=pltpu.VMEM)
    return pl.pallas_call(
        functools.partial(scatter_kernel, nz, count),
        out_shape=[jax.ShapeDtypeStruct(p.shape[4:], jnp.float32) for p in partials],
        in_specs=[vmem] * count, out_specs=[vmem] * count, scratch_shapes=scratch,
        compiler_params=pltpu.CompilerParams(collective_id=1, has_side_effects=True, vmem_limit_bytes=60 * 2**20),
        name="scatter_grads",
    )(*partials)


HEADS = 8
EPSILON = 1e-05
VMEM_LIMIT = 60 * 2**20


def dot(left, right):
    return jnp.dot(left, right, preferred_element_type=F32)


def dot_nt(left, right):
    return lax.dot_general(left, right, (((1,), (1,)), ((), ())), preferred_element_type=F32)


def norm_rows(values):
    count = values.shape[0]
    shifted = values - jnp.sum(values, axis=0, keepdims=True) * (1.0 / count)
    inverse = lax.rsqrt(jnp.sum(shifted * shifted, axis=0, keepdims=True) * (1.0 / count) + EPSILON)
    return shifted * inverse, inverse


def norm_rows_back(grad, gain, normed, inverse):
    count = grad.shape[0]
    scaled = grad * gain
    lean = jnp.sum(scaled, axis=0, keepdims=True) * (1.0 / count)
    turn = jnp.sum(scaled * normed, axis=0, keepdims=True) * (1.0 / count)
    return inverse * (scaled - lean - normed * turn)


def fold(values):
    total = values[:, :128]
    for k in range(1, values.shape[1] // 128):
        total = total + values[:, 128 * k:128 * (k + 1)]
    return total


def param(small, column):
    return small[:, column:column + 1].astype(F32)


def attention_forward(tokens, waves, small, time_w, w_qkv, w_out):
    seqs, _, length = tokens.shape
    feat = time_w.shape[0]
    head = feat // HEADS
    turn = math.log2(math.e) / math.sqrt(head)

    def kernel(tok_ref, waves_ref, small_ref, time_ref, qkv_ref, out_ref, start_o, middle_o, project_o, powers_o, inv_o, mixed_o, qkv_t, out_t, stamps):
        i = pl.program_id(0)

        @pl.when(i == 0)
        def _():
            qkv_t[...] = qkv_ref[...].T
            out_t[...] = out_ref[...].T
            stamps[...] = dot(time_ref[...].T, waves_ref[...])

        tok = tok_ref[0]
        one_hot = (lax.broadcasted_iota(jnp.int32, (128, length), 0) == tok).astype(BF16)
        lane = lax.broadcasted_iota(jnp.int32, stamps.shape, 1)
        stamp = jnp.sum(jnp.where(lane == i, stamps[...], 0.0), axis=1, keepdims=True)
        start = dot(small_ref[...], one_hot) + stamp
        start_o[...] = start
        normed, _ = norm_rows(start)
        low = (normed * param(small_ref[...], 27) + param(small_ref[...], 28)).astype(BF16)
        project_o[...] = dot(qkv_t[...], low).astype(BF16)
        for h in range(HEADS):
            rows = pl.ds(h * head, head)
            keys = project_o[pl.ds(feat + h * head, head), :].T
            scores = dot(keys, project_o[rows, :])
            top = jnp.max(scores, axis=0, keepdims=True)
            powers = jnp.exp2((scores - top) * turn)
            inverse = 1.0 / jnp.sum(powers, axis=0, keepdims=True)
            low_powers = powers.astype(BF16)
            powers_o[0, h] = low_powers
            inv_o[0, h:h + 1, :] = inverse
            mixed_o[rows, :] = (dot(project_o[pl.ds(2 * feat + h * head, head), :], low_powers) * inverse).astype(BF16)
        middle_o[...] = start + dot(out_t[...], mixed_o[...])

    whole = lambda a: pl.BlockSpec(a.shape, lambda i: (0,) * a.ndim)
    block = lambda rows: pl.BlockSpec((rows, length), lambda i: (0, i))
    n = seqs * length
    return pl.pallas_call(
        kernel, grid=(seqs,),
        in_specs=[pl.BlockSpec((1, 1, length), lambda i: (i, 0, 0))] + [whole(a) for a in (waves, small, time_w, w_qkv, w_out)],
        out_specs=[block(feat), block(feat), block(3 * feat), pl.BlockSpec((1, HEADS, length, length), lambda i: (i, 0, 0, 0)),
                   pl.BlockSpec((1, HEADS, length), lambda i: (i, 0, 0)), block(feat)],
        out_shape=[jax.ShapeDtypeStruct((feat, n), F32), jax.ShapeDtypeStruct((feat, n), F32), jax.ShapeDtypeStruct((3 * feat, n), BF16),
                   jax.ShapeDtypeStruct((seqs, HEADS, length, length), BF16), jax.ShapeDtypeStruct((seqs, HEADS, length), F32),
                   jax.ShapeDtypeStruct((feat, n), BF16)],
        scratch_shapes=[pltpu.VMEM((3 * feat, feat), BF16), pltpu.VMEM((feat, feat), BF16), pltpu.VMEM((feat, 128), F32)],
        compiler_params=pltpu.CompilerParams(vmem_limit_bytes=VMEM_LIMIT), name="attention_forward",
    )(tokens, waves, small, time_w, w_qkv, w_out)


def feed_forward(middle, cotangent, small, w_up, w_down, chunk=256):
    feat, n = middle.shape
    ff = w_up.shape[1]
    steps = n // chunk
    tile = 256

    def kernel(mid_ref, cot_ref, small_ref, up_ref, down_ref, result_o, grad_o, ln_o, dup_o, ddown_o,
               up_t, down_t, act, gh, cot_f, low_f):
        i = pl.program_id(0)

        @pl.when(i == 0)
        def _():
            up_t[...] = up_ref[...].T
            down_t[...] = down_ref[...].T
            ln_o[...] = jnp.zeros_like(ln_o)

        cols = pl.ds(pl.multiple_of(i * chunk, chunk), chunk)
        middle = mid_ref[...]
        normed, inverse = norm_rows(middle)
        gain = param(small_ref[...], 29)
        low = (normed * gain + param(small_ref[...], 30)).astype(BF16)
        low_f[:, cols] = low
        cot = cot_ref[...].T
        cot_f[:, cols] = cot
        for j in range(ff // tile):
            rows = pl.ds(j * tile, tile)
            hidden = dot(up_t[rows, :], low)
            grad_active = dot(down_ref[rows, :], cot).astype(BF16).astype(F32)
            cdf = 0.5 + 0.5 * lax.erf(hidden * math.sqrt(0.5))
            bell = jnp.exp2(hidden * hidden * (-0.5 * math.log2(math.e))) * (1.0 / math.sqrt(2.0 * math.pi))
            act[rows, cols] = (hidden * cdf).astype(BF16)
            gh[rows, cols] = (grad_active * (cdf + hidden * bell)).astype(BF16)
        result_o[...] = (middle + dot(down_t[...], act[:, cols])).T
        grad_normed = dot(up_ref[...], gh[:, cols])
        grad_o[...] = cot.astype(F32) + norm_rows_back(grad_normed, gain, normed, inverse)
        ln_o[0] += fold(grad_normed * normed)
        ln_o[1] += fold(grad_normed)

        @pl.when(i == steps - 1)
        def _():
            def up(j, _):
                rows = pl.ds(pl.multiple_of(j * tile, tile), tile)
                dup_o[:, rows] = dot_nt(low_f[...], gh[rows, :]).astype(BF16)
                ddown_o[rows, :] = dot_nt(act[rows, :], cot_f[...]).astype(BF16)
                return 0
            lax.fori_loop(0, ff // tile, up, 0)

    whole = lambda shape: pl.BlockSpec(shape, lambda i: (0,) * len(shape))
    return pl.pallas_call(
        kernel, grid=(steps,),
        in_specs=[pl.BlockSpec((feat, chunk), lambda i: (0, i)), pl.BlockSpec((chunk, feat), lambda i: (i, 0)),
                  whole(small.shape), whole(w_up.shape), whole(w_down.shape)],
        out_specs=[pl.BlockSpec((chunk, feat), lambda i: (i, 0)), pl.BlockSpec((feat, chunk), lambda i: (0, i)), whole((2, feat, 128)),
                   whole((feat, ff)), whole((ff, feat))],
        out_shape=[jax.ShapeDtypeStruct((n, feat), F32), jax.ShapeDtypeStruct((feat, n), F32), jax.ShapeDtypeStruct((2, feat, 128), F32),
                   jax.ShapeDtypeStruct((feat, ff), BF16), jax.ShapeDtypeStruct((ff, feat), BF16)],
        scratch_shapes=[pltpu.VMEM((ff, feat), BF16), pltpu.VMEM((feat, ff), BF16), pltpu.VMEM((ff, n), BF16), pltpu.VMEM((ff, n), BF16),
                        pltpu.VMEM((feat, n), BF16), pltpu.VMEM((feat, n), BF16)],
        compiler_params=pltpu.CompilerParams(vmem_limit_bytes=VMEM_LIMIT), name="feed_forward",
    )(middle, cotangent, small, w_up, w_down)


def attention_backward(tokens, waves, small, w_qkv, w_out, start, grad_middle, project, powers, inverses, mixed):
    seqs, _, length = tokens.shape
    feat, n = start.shape
    head = feat // HEADS
    scale = 1.0 / math.sqrt(head)

    def kernel(tok_ref, waves_ref, small_ref, qkv_ref, out_ref, start_ref, grad_ref, project_ref, powers_ref, inv_ref, mixed_ref,
               din_o, dqkv_o, dout_o, dtime_o, ln_o, dchar_o, ga_f, mix_f, low_f, gp_f, gs_f):
        i = pl.program_id(0)

        @pl.when(i == 0)
        def _():
            ln_o[...] = jnp.zeros_like(ln_o)
            dchar_o[...] = jnp.zeros_like(dchar_o)
            gs_f[...] = jnp.zeros_like(gs_f)

        cols = pl.ds(pl.multiple_of(i * length, length), length)
        grad_low = grad_ref[...].astype(BF16)
        ga_f[:, cols] = grad_low
        mix_f[:, cols] = mixed_ref[...]
        grad_mixed = dot(out_ref[...], grad_low).astype(BF16).astype(F32)
        for h in range(HEADS):
            rows = pl.ds(h * head, head)
            krows, vrows = pl.ds(feat + h * head, head), pl.ds(2 * feat + h * head, head)
            scaled = grad_mixed[h * head:(h + 1) * head] * inv_ref[0, h:h + 1, :]
            lean = jnp.sum(scaled * mixed_ref[rows, :].astype(F32), axis=0, keepdims=True)
            scaled = scaled.astype(BF16)
            low_powers = powers_ref[0, h]
            grad_probs = dot(project_ref[vrows, :].T, scaled)
            grad_scores = (low_powers.astype(F32) * (grad_probs - lean)).astype(BF16)
            gp_f[vrows, cols] = dot_nt(scaled, low_powers).astype(BF16)
            gp_f[rows, cols] = (dot(project_ref[krows, :], grad_scores) * scale).astype(BF16)
            gp_f[krows, cols] = (dot_nt(project_ref[rows, :], grad_scores) * scale).astype(BF16)
        normed, inverse = norm_rows(start_ref[...])
        gain = param(small_ref[...], 27)
        low_f[:, cols] = (normed * gain + param(small_ref[...], 28)).astype(BF16)
        grad_normed = dot(qkv_ref[...], gp_f[:, cols])
        din = grad_ref[...] + norm_rows_back(grad_normed, gain, normed, inverse)
        din_o[...] = din.T
        ln_o[0] += fold(grad_normed * normed)
        ln_o[1] += fold(grad_normed)
        lane = lax.broadcasted_iota(jnp.int32, gs_f.shape, 1)
        gs_f[...] += jnp.where(lane == i, jnp.sum(din, axis=1, keepdims=True), 0.0)
        one_hot = (lax.broadcasted_iota(jnp.int32, (128, length), 0) == tok_ref[0]).astype(BF16)
        high = din.astype(BF16)
        rest = (din - high.astype(F32)).astype(BF16)
        dchar_o[...] += dot_nt(high, one_hot) + dot_nt(rest, one_hot)

        @pl.when(i == seqs - 1)
        def _():
            dtime_o[...] = dot_nt(waves_ref[...], gs_f[...].astype(BF16)).astype(BF16)
            dout_o[...] = dot_nt(mix_f[...], ga_f[...]).astype(BF16)

            def one(j, _):
                rows = pl.ds(pl.multiple_of(j * 256, 256), 256)
                dqkv_o[:, rows] = dot_nt(low_f[...], gp_f[rows, :]).astype(BF16)
                return 0
            lax.fori_loop(0, 3 * feat // 256, one, 0)

    whole = lambda shape: pl.BlockSpec(shape, lambda i: (0,) * len(shape))
    block = lambda rows: pl.BlockSpec((rows, length), lambda i: (0, i))
    return pl.pallas_call(
        kernel, grid=(seqs,),
        in_specs=[pl.BlockSpec((1, 1, length), lambda i: (i, 0, 0)), whole(waves.shape), whole(small.shape), whole(w_qkv.shape), whole(w_out.shape),
                  block(feat), block(feat), block(3 * feat), pl.BlockSpec((1, HEADS, length, length), lambda i: (i, 0, 0, 0)),
                  pl.BlockSpec((1, HEADS, length), lambda i: (i, 0, 0)), block(feat)],
        out_specs=[pl.BlockSpec((length, feat), lambda i: (i, 0)), whole((feat, 3 * feat)), whole((feat, feat)), whole((feat, feat)),
                   whole((2, feat, 128)), whole((feat, 128))],
        out_shape=[jax.ShapeDtypeStruct((n, feat), F32), jax.ShapeDtypeStruct((feat, 3 * feat), BF16), jax.ShapeDtypeStruct((feat, feat), BF16),
                   jax.ShapeDtypeStruct((feat, feat), BF16), jax.ShapeDtypeStruct((2, feat, 128), F32), jax.ShapeDtypeStruct((feat, 128), F32)],
        scratch_shapes=[pltpu.VMEM((feat, n), BF16), pltpu.VMEM((feat, n), BF16), pltpu.VMEM((feat, n), BF16), pltpu.VMEM((3 * feat, n), BF16),
                        pltpu.VMEM((feat, 128), F32)],
        compiler_params=pltpu.CompilerParams(vmem_limit_bytes=VMEM_LIMIT), name="attention_backward",
    )(tokens, waves, small, w_qkv, w_out, start, grad_middle, project, powers, inverses, mixed)


def sinusoid(steps, features):
    half = features // 2
    frequency = jnp.exp(-math.log(10000.0) * jnp.arange(half, dtype=F32) / half)
    angles = frequency[:, None] * steps.astype(F32)[None, :]
    waves = jnp.concatenate([jnp.sin(angles), jnp.cos(angles)], axis=0).astype(BF16)
    return jnp.pad(waves, ((0, 0), (0, 128 - steps.shape[0])))


def pack_small(char_table, g1, b1, g2, b2):
    cols = jnp.concatenate([char_table.T, g1[:, None], b1[:, None], g2[:, None], b2[:, None]], axis=1)
    return jnp.pad(cols, ((0, 0), (0, 128 - cols.shape[1])))


def layer(tokens, timesteps, cotangent, small, time_w, w_qkv, w_out, w_up, w_down):
    seqs = timesteps.shape[0]
    tok = tokens.reshape(seqs, 1, tokens.shape[0] // seqs)
    waves = sinusoid(timesteps, time_w.shape[0])
    start, middle, project, powers, inv, mixed = attention_forward(tok, waves, small, time_w, w_qkv, w_out)
    result, grad_mid, ln2, dup, ddown = feed_forward(middle, cotangent, small, w_up, w_down)
    din, dqkv, dout, dtime, ln1, dchar = attention_backward(tok, waves, small, w_qkv, w_out, start, grad_mid, project, powers, inv, mixed)
    lns = jnp.sum(jnp.concatenate([ln1, ln2]), axis=-1)
    dsmall = jnp.concatenate([dchar[:, :27], lns.T, dchar[:, 31:]], axis=1)
    return result, din, dsmall, dtime, dqkv, dout, dup, ddown

AXES = ("gx", "gy")


def gather_all(mesh_shape, packed):
    count = mesh_shape[0] * mesh_shape[1]
    if mesh_shape[1] == 4 and mesh_shape[0] % 2 == 0 and all(p.shape[0] % 16 == 0 for p in packed):
        got = gather(mesh_shape[0] // 2, packed)
    else:
        got = [lax.all_gather(p, AXES, axis=0) for p in packed]
    return [g.reshape(count * p.shape[0], p.shape[1]) for g, p in zip(got, packed)]


def scatter_all(mesh_shape, parts):
    count = mesh_shape[0] * mesh_shape[1]
    rows = [p.shape[0] // count for p in parts]
    if mesh_shape[1] == 4 and mesh_shape[0] % 2 == 0 and all(r % 16 == 0 for r in rows):
        nz = mesh_shape[0] // 2
        return scatter(nz, [p.reshape(nz, 2, 2, 2, r, p.shape[1]) for p, r in zip(parts, rows)])
    return [lax.psum_scatter(p.astype(F32), AXES, scatter_dimension=0, tiled=True) for p in parts]


def make_body(mesh_shape):
    def body(tokens, timesteps, cotangent, char_table, time_weight, ln1_gain, ln1_bias, w_qkv, w_attn_out, ln2_gain, ln2_bias, w_up, w_down):
        feat = w_up.shape[0] * mesh_shape[0] * mesh_shape[1]
        ff = w_up.shape[1]
        chars = char_table.shape[0]
        small = pack_small(char_table, ln1_gain, ln1_bias, ln2_gain, ln2_bias)
        first, second, down = gather_all(mesh_shape, [
            jnp.concatenate([small, time_weight, w_qkv], axis=1), jnp.concatenate([w_attn_out, w_up], axis=1), w_down])
        result, din, dsmall, dtime, dqkv, dout, dup, ddown = layer(
            tokens, timesteps, cotangent, first[:, :128], first[:, 128:128 + feat], first[:, 128 + feat:], second[:, :feat], second[:, feat:], down)
        dup, ddown, rest = scatter_all(mesh_shape, [
            dup, ddown, jnp.concatenate([dsmall.astype(BF16), dtime, dqkv, dout], axis=1)])
        ln = rest[:, chars:chars + 4].T
        return (result, din, rest[:, :chars].T, rest[:, 128:128 + feat], ln[0], ln[1], rest[:, 128 + feat:128 + 4 * feat], rest[:, 128 + 4 * feat:],
                ln[2], ln[3], dup, ddown)
    return body


def solution(mesh):
    every = P(AXES)
    rows, cols = P(AXES, None), P(None, AXES)
    return jax.shard_map(
        make_body((mesh.shape["gx"], mesh.shape["gy"])),
        mesh=mesh,
        in_specs=(every, every, rows, cols, rows, every, every, rows, rows, every, every, rows, rows),
        out_specs=(rows, rows, cols, rows, every, every, rows, rows, every, every, rows, rows),
        check_vma=False,
    )
```

time: 1230 us -> 256 us (0.21)
  waiting for transfers between devices: 699 us -> 0 us
  Pallas kernels: 0 us -> 221 us
  blocking collectives: 200 us -> 0 us
  matrix products: 199 us -> 0 us
  local copies, waits for them, and re-layouts: 79.2 us -> 27.8 us
  other arithmetic: 30.9 us -> 6.19 us
  between operations: 14.9 us -> 0.75 us
    reduce_scatter x6 -> x0, waiting for transfers between devices: 697 us -> none  [the longest x1 143 us: body(): lax.psum_scatter(ffn_grads[2], ('gx', 'gy'), scatter_dimension=0, tiled=T...]
    pallas_call x0 -> x5, Pallas kernels: none -> 221 us  [the longest x1 53.6 us: scatter(): pl.pallas_call(functools.partial(scatter_kernel, nz, count), out_shape=[j...]
    dot_general x23 -> x0, matrix products: 199 us -> none  [the longest x1 44.2 us: ffn_parts(): hidden = jnp.dot(normed_low, up_weight, preferred_element_type=jnp.float32)]
    all_gather x3 -> x0, blocking collectives: 126 us -> none  [the longest x1 45 us: body(): lax.all_gather(time_weight, ('gx', 'gy'), axis=0, tiled=True)]
    unnamed x2 -> x0, blocking collectives: 74.4 us -> none
    unnamed x102 -> x8, local copies, waits for them, and re-layouts: 34.5 us -> 3.15 us
    reshape x3 -> x0, local copies, waits for them, and re-layouts: 25.1 us -> none  [the longest x1 16.3 us: attention_parts(): project.reshape(seq_count, start.shape[0] // seq_count, 3, HEADS, head_size)]
    convert_element_type x6 -> x1, other arithmetic: 13.1 us -> 0.66 us  [sinusoid(): angles = frequency[:, None] * steps.astype(F32)[None, :]]
  transfers between devices with their start and end apart: 9 -> 0, of which waited for: 6 -> 0; matrix products, arithmetic and copies ran while one was open for 16% -> 0% of each run, Pallas kernels for 0% -> 0%
where the time goes in v1:
time: 256 us; the launch traced here: 255 us
  Pallas kernels  221 us (86%)
  local copies, waits for them, and re-layouts  27.8 us (11%)
  other arithmetic  6.19 us (2%)
    pallas_call x1, Pallas kernels, scatter(): pl.pallas_call(functools.partial(scatter_kernel, nz, count), out_shape=[j...  53.6 us
    pallas_call x1, Pallas kernels, gather(): pl.pallas_call(functools.partial(gather_kernel, nz, count), out_shape=[ja...  51.7 us
    pallas_call x1, Pallas kernels, feed_forward(): pl.pallas_call(kernel, grid=(steps,), in_specs=[pl.BlockSpec((feat, chunk...  41.7 us
    pallas_call x1, Pallas kernels, attention_backward(): pl.pallas_call(kernel, grid=(seqs,), in_specs=[pl.BlockSpec((1, 1, length...  39.2 us
    pallas_call x1, Pallas kernels, attention_forward(): pl.pallas_call(kernel, grid=(seqs,), in_specs=[pl.BlockSpec((1, 1, length...  34.6 us
    concatenate x1, local copies, waits for them, and re-layouts, body(): jnp.concatenate([dsmall.astype(BF16), dtime, dqkv, dout], axis=1)  5.15 us

profile of v1, /device:TPU:0, one launch (start us, length us, event | category | flops | bytes accessed | tf_op | source)
XLA Modules:
  0.0 255.5 jit_solution(5039115710835318201)
XLA Ops:
  0.6 0.7 convert_element_type.6
  1.3 0.7 copy.34
  2.1 0.7 copy.35
  2.8 0.7 copy.36
  3.5 0.7 copy.37
  4.3 0.8 concatenate.23
  5.1 0.1 fusion.3
  5.2 1.4 fusion.2.refs_0_
  6.6 1.5 pad_maximum_fusion.refs_1_
  8.1 0.2 copy.33
  8.3 0.7 pad.8.waves_ref
  9.0 51.7 %gather_weights.1 = (bf16[4,2,2,2,16,2176]{5,4,3,2,1,0:T(8,128)(2,1)}, bf16[4,2,2,2,16,2560]{5,4,3,2,1,0:T(8,128)(2,1)}, bf16[4,2,2,2,64,512]{5,4,3,2,1,0:T(8,128)(2,1)}) custom-call(bf16[16,2176]{1,0:T(8,128)(2,1)} %fusion.2.refs_0_, bf16[16,2560]{1,0:T(8,128)(2,1)} %pad_maximum_fusion.refs_1_, bf16[64,512]{1,0:T(8,128)(2,1)} %refs_2_.1), custom_call_target="tpu_custom_call" | custom-call | tf_op jit(solution)/shard_map/gather_weights/pallas_call | solution.py:166
  60.7 1.6 slice.66.small_ref
  62.2 2.0 slice.69.out_ref
  64.3 3.2 %slice.70.up_ref = bf16[512,2048]{1,0:T(8,128)(2,1)} slice(bf16[512,2560]{1,0:T(8,128)(2,1)} %bitcast.20), slice={[0:512], [512:2560]} | slice | bytes 4194304 | tf_op jit(solution)/shard_map/slice | solution.py:607
  67.4 0.8 slice.67.time_ref
  68.3 1.2 slice.68.qkv_ref
  69.5 34.6 %attention_forward.1 = (f32[512,2048]{1,0:T(8,128)}, f32[512,2048]{1,0:T(8,128)}, bf16[1536,2048]{1,0:T(8,128)(2,1)}, bf16[8,8,256,256]{3,2,1,0:T(8,128)(2,1)}, ...) custom-call(s32[8,1,256]{2,1,0:T(1,128)} %bitcast.29, bf16[512,128]{1,0:T(8,128)(2,1)} %pad.8.waves_ref, ...), custom_call_target="tpu_custom_call" | custom-call | tf_op jit(solution)/shard_map/attention_forward/pallas_call | solution.py:402
  104.1 41.7 %feed_forward.1 = (f32[2048,512]{1,0:T(8,128)}, f32[512,2048]{1,0:T(8,128)}, f32[2,512,128]{2,1,0:T(8,128)}, bf16[512,2048]{1,0:T(8,128)(2,1)}, bf16[2048,512]{1,0:T(8,128)(2,1)}) custom-call(f32[512,2048]{1,0:T(8,128)} %get-tuple-element.37.mid_ref, bf16[2048,512]{1,0:T(8,128)(2,1)} %cot_ref.1, bf16[512,128]{1,0:T(8,128)(2,1)} %slice.66.small_ref, ...), custom_call_target="tpu_custom_call" | custom-call | tf_op jit(solution)/shard_map/feed_forward/pallas_call | solution.py:463
  145.8 39.2 %attention_backward.1 = (f32[2048,512]{1,0:T(8,128)}, bf16[512,1536]{1,0:T(8,128)(2,1)}, bf16[512,512]{1,0:T(8,128)(2,1)}, bf16[512,512]{1,0:T(8,128)(2,1)}, f32[2,512,128]{2,1,0:T(8,128)}, /*index=5*/f32[512,128]{1,0:T(8,128)}) custom-call(s32[8,1,256]{2,1,0:T(1,128)} %bitcast.30, bf16[512,128]{1,0:T(8,128)(2,1)} %pad.8.waves_ref, ...), custom_call_target="tpu_custom_call" | custom-call | tf_op jit(solution)/shard_map/attention_backward/pallas_call | solution.py:538
  185.1 1.5 maximum_reduce_fusion
  186.6 0.2 copy.38
  186.8 1.0 convert.18
  187.8 5.2 %concatenate.27 = bf16[512,2688]{1,0:T(8,128)(2,1)} concatenate(bf16[512,27]{1,0:T(8,128)(2,1)S(1)} %bitcast.27, bf16[512,4]{1,0:T(8,128)(2,1)S(1)} %bitcast.28, bf16[512,97]{1,0:T(8,128)(2,1)S(1)} %slice.72, bf16[512,512]{1,0:T(8,128)(2,1)} %get-tuple-element.52, bf16[512,1536]{1,0:T(8,128)(2,1)S(1)} %copy-done.1, bf16[512,512]{1,0:T(8,128)(2,1)} %get-tuple-element.54), dimensions={1} | concatenate | bytes 5505024 | tf_op jit(solution)/shard_map/concatenate | solution.py:609
  193.0 53.6 %scatter_grads.1 = (f32[16,2048]{1,0:T(8,128)}, f32[64,512]{1,0:T(8,128)}, f32[16,2688]{1,0:T(8,128)}) custom-call(bf16[4,2,2,2,16,2048]{5,4,3,2,1,0:T(8,128)(2,1)} %bitcast.24, bf16[4,2,2,2,64,512]{5,4,3,2,1,0:T(8,128)(2,1)} %bitcast.25, bf16[4,2,2,2,16,2688]{5,4,3,2,1,0:T(8,128)(2,1)} %bitcast.18), custom_call_target="tpu_custom_call" | custom-call | tf_op jit(solution)/shard_map/scatter_grads/pallas_call | solution.py:314
  246.6 0.8 slice_bitcast_fusion
  247.4 0.7 slice_reduce_fusion
  248.1 1.3 slice_bitcast_fusion.1
  249.4 1.4 fusion.5
  250.8 1.5 slice.62
  252.3 1.6 copy.41
  253.9 1.6 copy.42
  (9 shorter events, 0.1 us)
Async XLA Ops:
  62.2 5.2 %copy-start = (bf16[4,2,2,2,16,2176]{5,4,3,2,1,0:T(8,128)(2,1)S(1)}, bf16[4,2,2,2,16,2176]{5,4,3,2,1,0:T(8,128)(2,1)}, u32[]{:S(2)}) copy-start(bf16[4,2,2,2,16,2176]{5,4,3,2,1,0:T(8,128)(2,1)} %get-tuple-element.35) | copy-start | bytes 6684676
  145.8 39.2 %copy-start.2 = (f32[2,512,128]{2,1,0:T(8,128)S(1)}, f32[2,512,128]{2,1,0:T(8,128)}, u32[]{:S(2)}) copy-start(f32[2,512,128]{2,1,0:T(8,128)} %get-tuple-element.51) | copy-start | bytes 1572868
  185.0 2.8 %copy-start.1 = (bf16[512,1536]{1,0:T(8,128)(2,1)S(1)}, bf16[512,1536]{1,0:T(8,128)(2,1)}, u32[]{:S(2)}) copy-start(bf16[512,1536]{1,0:T(8,128)(2,1)} %get-tuple-element.53) | copy-start | bytes 4718596

commit v2 on v0

v2 whole, which is shorter than its diff:
```python
import types
import math

import jax
import jax.numpy as jnp
from jax import lax
from jax.experimental import pallas as pl
from jax.experimental.pallas import tpu as pltpu
from jax.sharding import PartitionSpec as P

F32, BF16 = jnp.float32, jnp.bfloat16

MESH = pl.DeviceIdType.MESH


def place():
    gx, gy = lax.axis_index("gx"), lax.axis_index("gy")
    return gx // 2, gx % 2, gy // 2, gy % 2


def device(z, x, y, c):
    return (z * 2 + x, y * 2 + c)


def greet(nz):
    z, x, y, c = place()
    barrier = pltpu.get_barrier_semaphore()
    for where in [(z, x, y, 1 - c), (z, 1 - x, y, c), (z, x, 1 - y, c)] + [((z + d) % nz, x, y, c) for d in range(1, nz)]:
        pl.semaphore_signal(barrier, inc=1, device_id=device(*where), device_id_type=MESH)


def greeted(nz):
    pl.semaphore_wait(pltpu.get_barrier_semaphore(), 3 + nz - 1)


def send(src, dst, sems, slot, where):
    return pltpu.make_async_remote_copy(
        src_ref=src, dst_ref=dst, send_sem=sems.at[0, slot], recv_sem=sems.at[1, slot],
        device_id=device(*where), device_id_type=MESH)


def middle_of(width):
    return width // 256 * 128


class Gather:
    NAMES = ("x", "y", "xd", "yd", "c0", "c1", "c2", "c3", "c4")

    @staticmethod
    def scratch(nz):
        return pltpu.SemaphoreType.DMA((2, nz - 1 + 9))

    def __init__(self, nz, shard, out, sems):
        self.nz, self.shard, self.out, self.sems = nz, shard, out, sems

    def along(self, d, comes=False):
        z, x, y, c = place()
        come = (z + self.nz - d) % self.nz
        return send(self.shard, self.out.at[come if comes else z, x, y, c], self.sems, d - 1, ((z + d) % self.nz, x, y, c))

    def copy(self, name, comes=False):
        z, x, y, c = place()
        width = self.out.shape[-1]
        lo, hi = pl.ds(0, middle_of(width)), pl.ds(middle_of(width), width - middle_of(width))
        to, a, b, k, cut, slot = {
            "x": ("x", x, y, c, None, 0), "y": ("y", x, y, c, None, 1),
            "xd": ("x", x, 1 - y, c, lo, 2), "yd": ("y", 1 - x, y, c, hi, 3),
            "c0": ("c", x, y, c, None, 4), "c1": ("c", 1 - x, y, c, None, 5), "c2": ("c", x, 1 - y, c, None, 6),
            "c3": ("c", 1 - x, 1 - y, c, lo, 7), "c4": ("c", 1 - x, 1 - y, c, hi, 8)}[name]
        if comes:
            a, b, k = (1 - a, b, k) if to == "x" else (a, 1 - b, k) if to == "y" else (a, b, 1 - k)
        where = {"x": (z, 1 - x, y, c), "y": (z, x, 1 - y, c), "c": (z, x, y, 1 - c)}[to]
        ref = self.out.at[pl.ds(0, self.nz), a, b, k]
        if cut is not None:
            ref = ref.at[:, :, cut]
        return send(ref, ref, self.sems, self.nz - 1 + slot, where)

    def start(self, *names):
        for name in names:
            self.copy(name).start()

    def arrive(self, *names):
        for name in names:
            self.copy(name, comes=True).wait_recv()

    def lines(self):
        for d in range(1, self.nz):
            self.along(d).start()

    def sides(self):
        for d in range(1, self.nz):
            self.along(d, comes=True).wait_recv()
        self.start("x", "y", "c0")

    def corners(self):
        self.arrive("x", "y")
        self.start("xd", "yd", "c1", "c2")

    def cores(self):
        self.arrive("xd", "yd")
        self.start("c3", "c4")

    def whole(self):
        self.arrive("c0", "c1", "c2", "c3", "c4")

    def finish(self):
        for d in range(1, self.nz):
            self.along(d).wait_send()
        for name in self.NAMES:
            self.copy(name).wait_send()


class Scatter:
    @staticmethod
    def scratch(nz, tail, dtype):
        return [pltpu.VMEM((nz, 2, 2) + tail, dtype), pltpu.VMEM((nz,) + tail, dtype), pltpu.VMEM((2, nz) + tail, dtype),
                pltpu.VMEM((nz - 1,) + tail, dtype), pltpu.SemaphoreType.DMA((2, nz - 1 + 5))]

    def __init__(self, nz, mine, kept, own, far, near, line, sems):
        self.nz, self.mine, self.kept, self.own, self.far, self.near, self.line, self.sems = nz, mine, kept, own, far, near, line, sems
        self.width = own.shape[-1]

    def copy(self, name):
        z, x, y, c = place()
        nz, own, sems, base = self.nz, self.own, self.sems, self.nz - 1
        half = middle_of(self.width)
        lo, hi = pl.ds(0, half), pl.ds(half, self.width - half)
        all_z = pl.ds(0, nz)
        xp, yp, cp = (z, 1 - x, y, c), (z, x, 1 - y, c), (z, x, y, 1 - c)
        if name == "c":
            return send(self.mine.at[all_z, :, :, 1 - c], own, sems, base, cp)
        if name == "xd":
            return send(own.at[all_z, 1 - x, 1 - y, :, lo], self.far.at[:, :, lo], sems, base + 1, xp)
        if name == "yd":
            return send(own.at[all_z, 1 - x, 1 - y, :, hi], self.far.at[:, :, hi], sems, base + 2, yp)
        if name == "x":
            return send(own.at[all_z, 1 - x, y], self.near.at[0], sems, base + 3, xp)
        return send(own.at[all_z, x, 1 - y], self.near.at[1], sems, base + 4, yp)

    def along(self, d):
        z, x, y, c = place()
        to = (z + d) % self.nz
        return send(self.own.at[to, x, y], self.line.at[d - 1], self.sems, d - 1, (to, x, y, c))

    def add(self, a, b, *values, cut=None):
        cols = cut if cut is not None else pl.ds(0, self.width)

        def one(k, _):
            spot = (k, a, b, slice(None), cols)
            total = self.own[spot]
            for value in values:
                total = total + value(k, cols)
            self.own[spot] = total
            return 0
        lax.fori_loop(0, self.nz, one, 0)

    def cores(self):
        self.copy("c").start()

    def corners(self):
        z, x, y, c = place()
        self.copy("c").wait()
        for a, b in ((1 - x, 1 - y), (1 - x, y), (x, 1 - y), (x, y)):
            self.add(a, b, lambda k, cols, a=a, b=b: self.kept(k, a, b, cols))
            if a is not x and b is not y:
                self.copy("xd").start()
                self.copy("yd").start()

    def sides(self):
        z, x, y, c = place()
        half = middle_of(self.width)
        self.copy("xd").wait()
        self.add(x, 1 - y, lambda k, cols: self.far[k, :, cols], cut=pl.ds(0, half))
        self.copy("y").start()
        self.copy("yd").wait()
        self.add(1 - x, y, lambda k, cols: self.far[k, :, cols], cut=pl.ds(half, self.width - half))
        self.copy("x").start()

    def lines(self):
        z, x, y, c = place()
        self.copy("x").wait()
        self.copy("y").wait()
        self.add(x, y, lambda k, cols: self.near[0, k, :, cols], lambda k, cols: self.near[1, k, :, cols])
        for d in range(1, self.nz):
            self.along(d).start()

    def total(self):
        z, x, y, c = place()
        for d in range(1, self.nz):
            self.along(d).wait()
        total = self.own[z, x, y].astype(F32)
        for d in range(1, self.nz):
            total = total + self.line[d - 1].astype(F32)
        return total

HEADS = 8
EPSILON = 1e-05
VMEM_LIMIT = 62 * 2**20
BLOCKS = (2, 2, 2)


def dot(left, right):
    return jnp.dot(left, right, preferred_element_type=F32)


def dot_nt(left, right):
    return lax.dot_general(left, right, (((1,), (1,)), ((), ())), preferred_element_type=F32)


def norm_rows(values):
    count = values.shape[0]
    shifted = values - jnp.sum(values, axis=0, keepdims=True) * (1.0 / count)
    inverse = lax.rsqrt(jnp.sum(shifted * shifted, axis=0, keepdims=True) * (1.0 / count) + EPSILON)
    return shifted * inverse, inverse


def norm_rows_back(grad, gain, normed, inverse):
    count = grad.shape[0]
    scaled = grad * gain
    lean = jnp.sum(scaled, axis=0, keepdims=True) * (1.0 / count)
    turn = jnp.sum(scaled * normed, axis=0, keepdims=True) * (1.0 / count)
    return inverse * (scaled - lean - normed * turn)


def fold(values):
    total = values[:, :128]
    for k in range(1, values.shape[1] // 128):
        total = total + values[:, 128 * k:128 * (k + 1)]
    return total


def flat(ref, cols=slice(None)):
    value = ref[(slice(None),) * (len(ref.shape) - 1) + (cols,)]
    return value.reshape(-1, value.shape[-1])


class Call:
    def __init__(self):
        self.ins, self.outs, self.scratch = [], [], []

    def arg(self, name, array, spec):
        self.ins.append((name, array, spec))

    def out(self, name, shape, dtype, spec):
        self.outs.append((name, jax.ShapeDtypeStruct(shape, dtype), spec))

    def temp(self, name, kind):
        self.scratch.append((name, kind))

    def run(self, kernel, name, grid, collective=None):
        names = [n for n, *_ in self.ins + self.outs + self.scratch]

        def body(*refs):
            kernel(types.SimpleNamespace(**dict(zip(names, refs))))
        extra = {} if collective is None else dict(collective_id=collective, has_side_effects=True)
        got = pl.pallas_call(
            body, grid=grid, in_specs=[s for *_, s in self.ins], out_specs=[s for *_, s in self.outs],
            out_shape=[s for _, s, _ in self.outs], scratch_shapes=[k for _, k in self.scratch],
            compiler_params=pltpu.CompilerParams(vmem_limit_bytes=VMEM_LIMIT, **extra), name=name,
        )(*[a for _, a, _ in self.ins])
        return dict(zip([n for n, *_ in self.outs], got))


def whole(shape):
    return pl.BlockSpec(tuple(shape), lambda i: (0,) * len(shape))


def lanes(rows, width, first=0):
    return pl.BlockSpec((rows, width), lambda i: (0, jnp.maximum(i - first, 0)))


ANYWHERE = pl.BlockSpec(memory_space=pl.ANY)


def fill_waves(r, feat):
    half = feat // 2
    r.steps_row[...] = jnp.zeros_like(r.steps_row)
    r.steps_row[:, :r.steps.shape[1]] = r.steps[...].astype(F32)
    rate = jnp.exp(lax.broadcasted_iota(jnp.int32, (half, 128), 0).astype(F32) * (-math.log(10000.0) / half))
    angles = rate * r.steps_row[...]
    r.waves[:half, :] = jnp.sin(angles).astype(BF16)
    r.waves[half:, :] = jnp.cos(angles).astype(BF16)


def fill_small(r, chars):
    r.square[...] = jnp.zeros_like(r.square)
    count = r.char.shape[1]
    r.square[:chars, :count] = r.char[...].astype(F32)
    for k, ref in enumerate((r.g1, r.b1, r.g2, r.b2)):
        r.square[chars + k:chars + k + 1, :count] = ref[...].astype(F32)
    r.small_shard[...] = r.square[...].T[:count].astype(BF16)


def param(r, column):
    return r[:, column:column + 1].astype(F32)


def embed(r, i, tok, small):
    one_hot = (lax.broadcasted_iota(jnp.int32, (128, tok.shape[1]), 0) == tok).astype(BF16)
    lane = lax.broadcasted_iota(jnp.int32, r.stamps.shape, 1)
    stamp = jnp.sum(jnp.where(lane == i, r.stamps[...], 0.0), axis=1, keepdims=True)
    return dot(small, one_hot) + stamp


def heads_forward(r, feat):
    head = feat // HEADS
    turn = math.log2(math.e) / math.sqrt(head)
    rows = [pl.ds(h * head, head) for h in range(HEADS)]
    for h in range(HEADS):
        r.scores[h] = dot(r.project[pl.ds(feat + h * head, head), :].T, r.project[rows[h], :])
    for h in range(HEADS):
        scores = r.scores[h]
        powers = jnp.exp2((scores - jnp.max(scores, axis=0, keepdims=True)) * turn)
        r.inv[0, h:h + 1, :] = 1.0 / jnp.sum(powers, axis=0, keepdims=True)
        r.powers[0, h] = powers.astype(BF16)
    for h in range(HEADS):
        mixed = dot(r.project[pl.ds(2 * feat + h * head, head), :], r.powers[0, h])
        r.mixed[rows[h], :] = (mixed * r.inv[0, h:h + 1, :]).astype(BF16)


def attention_forward(nz, tokens, timesteps, shards):
    char, g1, b1, g2, b2, time_w, w_qkv, w_out, w_up, w_down = shards
    seqs = timesteps.shape[0]
    n = tokens.shape[0]
    length = n // seqs
    feat = time_w.shape[1]
    ff = w_up.shape[1]
    chars = char.shape[0]
    count = char.shape[1]
    call = Call()
    call.arg("tok", tokens.reshape(seqs, 1, length), whole((seqs, 1, length)))
    call.arg("steps", timesteps.reshape(1, seqs), whole((1, seqs)))
    call.arg("char", char, whole(char.shape))
    for name, value in (("g1", g1), ("b1", b1), ("g2", g2), ("b2", b2)):
        call.arg(name, value.reshape(1, count), whole((1, count)))
    call.arg("time_w", time_w, whole(time_w.shape))
    call.arg("w_qkv", w_qkv, whole(w_qkv.shape))
    call.arg("w_out", w_out, whole(w_out.shape))
    if nz:
        call.arg("w_up", w_up, ANYWHERE)
        call.arg("w_down", w_down, ANYWHERE)
    for name, rows, kind in (("start", feat, F32), ("middle", feat, F32), ("project", 3 * feat, BF16), ("mixed", feat, BF16)):
        call.out(name, (rows, n), kind, lanes(rows, length))
    call.out("powers", (seqs, HEADS, length, length), BF16, pl.BlockSpec((1, HEADS, length, length), lambda i: (i, 0, 0, 0)))
    call.out("inv", (seqs, HEADS, length), F32, pl.BlockSpec((1, HEADS, length), lambda i: (i, 0, 0)))
    call.out("waves", (feat, 128), BF16, whole((feat, 128)))
    parts = 3
    if nz:
        blocks = lambda a: (nz,) + BLOCKS + a
        kept = {"first": (count, 128 + feat), "out": w_out.shape}
        kept.update({f"qkv{p}": (count, feat) for p in range(parts)})
        for name, tail in kept.items():
            call.temp(name, pltpu.VMEM(blocks(tail), BF16))
            call.temp(name + "_sems", Gather.scratch(nz))
        for name, tail in (("up", w_up.shape), ("down", w_down.shape)):
            call.out(name, blocks(tail), BF16, ANYWHERE)
            call.temp(name + "_sems", Gather.scratch(nz))
        for name, tail in (("first_o", kept["first"]), ("out_o", kept["out"]), ("qkv_o", w_qkv.shape)):
            call.out(name, blocks(tail), BF16, ANYWHERE)
        call.temp("first_shard", pltpu.VMEM((count, 128 + feat), BF16))
        call.temp("place_sems", pltpu.SemaphoreType.DMA((2,)))
        call.temp("save_sems", pltpu.SemaphoreType.DMA((2 + parts,)))
    else:
        call.out("small", (count, 128), BF16, whole((count, 128)))
    call.temp("small_shard", pltpu.VMEM((count, 128), BF16))
    call.temp("square", pltpu.VMEM((128, max(count, 128)), F32))
    call.temp("steps_row", pltpu.VMEM((1, 128), F32))
    call.temp("stamps", pltpu.VMEM((feat, 128), F32))
    call.temp("qkv_t", pltpu.VMEM((3 * feat, feat), BF16))
    call.temp("out_t", pltpu.VMEM((feat, feat), BF16))
    call.temp("starts", pltpu.VMEM((seqs, feat, length), F32))
    call.temp("low", pltpu.VMEM((seqs, feat, length), BF16))
    call.temp("scores", pltpu.VMEM((HEADS, length, length), F32))

    def kernel(r):
        i = pl.program_id(0)
        if nz:
            z, x, y, c = place()
            first = Gather(nz, r.first_shard, r.first, r.first_sems)
            qkv = [Gather(nz, r.w_qkv.at[:, pl.ds(p * feat, feat)], getattr(r, f"qkv{p}"), getattr(r, f"qkv{p}_sems")) for p in range(parts)]
            out = Gather(nz, r.w_out, r.out, r.out_sems)
            up = Gather(nz, r.w_up, r.up, r.up_sems)
            down = Gather(nz, r.w_down, r.down, r.down_sems)
            put = [pltpu.make_async_copy(g.shard, g.out.at[z, x, y, c], r.place_sems.at[k]) for k, g in enumerate((up, down))]
            every = (pl.ds(0, nz), slice(None), slice(None), slice(None), slice(None))
            save = [pltpu.make_async_copy(r.first, r.first_o, r.save_sems.at[0]), pltpu.make_async_copy(r.out, r.out_o, r.save_sems.at[1])]
            save += [pltpu.make_async_copy(g.out, r.qkv_o.at[every + (pl.ds(p * feat, feat),)], r.save_sems.at[2 + p]) for p, g in enumerate(qkv)]

        def small():
            return flat(r.first, slice(0, 128)) if nz else r.small[...]

        def begin(some):
            table = small()
            for k in some:
                start = embed(r, k, r.tok[k], table)
                r.starts[k] = start
                normed, _ = norm_rows(start)
                r.low[k] = (normed * param(table, chars) + param(table, chars + 1)).astype(BF16)

        @pl.when(i == 0)
        def _():
            if nz:
                greet(nz)
                for copy in put:
                    copy.start()
            fill_small(r, chars)
            if nz:
                q, k, v = qkv
                r.first_shard[:, :128] = r.small_shard[...]
                r.first_shard[:, 128:] = r.time_w[...]
                for g in (first, out, q, k, v):
                    g.out[z, x, y, c] = g.shard[...]
                greeted(nz)
                first.lines()
                q.lines()
                fill_waves(r, feat)
                first.sides()
                k.lines()
                q.sides()
                v.lines()
                first.corners()
                k.sides()
                out.lines()
                q.corners()
                first.cores()
                v.sides()
                k.corners()
                q.cores()
                first.whole()
                r.stamps[...] = dot(flat(r.first, slice(128, 128 + feat)).T, r.waves[...])
                out.sides()
                v.corners()
                k.cores()
                begin(range(0, seqs // 2))
                out.corners()
                v.cores()
                q.whole()
                r.qkv_t[:feat] = flat(r.qkv0).T
                up.lines()
                begin(range(seqs // 2, seqs))
                out.cores()
                k.whole()
                r.qkv_t[feat:2 * feat] = flat(r.qkv1).T
                v.whole()
                r.qkv_t[2 * feat:] = flat(r.qkv2).T
            else:
                r.small[...] = r.small_shard[...]
                fill_waves(r, feat)
                r.stamps[...] = dot(r.time_w[...].T, r.waves[...])
                r.qkv_t[...] = r.w_qkv[...].T
                r.out_t[...] = r.w_out[...].T
                begin(range(seqs))

        r.project[...] = dot(r.qkv_t[...], r.low[i]).astype(BF16)
        heads_forward(r, feat)
        if nz:
            @pl.when(i == 0)
            def _():
                out.whole()
                r.out_t[...] = flat(r.out).T
                for copy in put:
                    copy.wait()
                up.sides()
                down.lines()
                for copy in save:
                    copy.start()

            @pl.when(i == 2)
            def _():
                down.sides()

            @pl.when(i == 3)
            def _():
                up.corners()

            @pl.when(i == 5)
            def _():
                up.cores()
                down.corners()

            @pl.when(i == seqs - 1)
            def _():
                down.cores()
                for copy in save:
                    copy.wait()
                for g in (up, down):
                    g.whole()
                for g in (first, *qkv, out, up, down):
                    g.finish()
        start = r.starts[i]
        r.start[...] = start
        r.middle[...] = start + dot(r.out_t[...], r.mixed[...])

    return call.run(kernel, "attention_forward", (seqs,), 0 if nz else None)


def feed_forward(chars, middle, cotangent, mixed, small, w_up, w_down, chunk=512):
    feat, n = middle.shape
    ff = w_up.shape[1]
    steps = n // chunk
    tile = 256
    call = Call()
    call.arg("middle", middle, lanes(feat, chunk))
    call.arg("cot", cotangent, pl.BlockSpec((chunk, feat), lambda i: (i, 0)))
    call.arg("mixed", mixed, whole(mixed.shape))
    call.arg("small", small, whole((feat, 128)))
    call.arg("w_up", w_up, whole(w_up.shape))
    call.arg("w_down", w_down, whole(w_down.shape))
    call.out("result", (n, feat), F32, pl.BlockSpec((chunk, feat), lambda i: (i, 0)))
    call.out("grad", (feat, n), F32, lanes(feat, chunk))
    call.out("ln", (2, feat, 128), F32, whole((2, feat, 128)))
    call.out("d_up", (feat, ff + feat), BF16, whole((feat, ff + feat)))
    call.out("d_down", (ff, feat), BF16, whole((ff, feat)))
    call.temp("up_t", pltpu.VMEM((ff, feat), BF16))
    call.temp("down_t", pltpu.VMEM((feat, ff), BF16))
    call.temp("act", pltpu.VMEM((ff, n), BF16))
    call.temp("gh", pltpu.VMEM((ff, n), BF16))
    call.temp("cot_f", pltpu.VMEM((feat, n), BF16))
    call.temp("low_f", pltpu.VMEM((feat, n), BF16))
    call.temp("ga_f", pltpu.VMEM((feat, n), BF16))

    def kernel(r):
        i = pl.program_id(0)

        @pl.when(i == 0)
        def _():
            r.up_t[...] = r.w_up[...].T
            r.down_t[...] = r.w_down[...].T
            r.ln[...] = jnp.zeros_like(r.ln)

        cols = pl.ds(pl.multiple_of(i * chunk, chunk), chunk)
        middle = r.middle[...]
        normed, inverse = norm_rows(middle)
        gain = param(r.small, chars + 2)
        low = (normed * gain + param(r.small, chars + 3)).astype(BF16)
        r.low_f[:, cols] = low
        cot = r.cot[...].T
        r.cot_f[:, cols] = cot
        for j in range(ff // tile):
            rows = pl.ds(j * tile, tile)
            hidden = dot(r.up_t[rows, :], low)
            grad_active = dot(r.w_down[rows, :], cot).astype(BF16).astype(F32)
            cdf = 0.5 + 0.5 * lax.erf(hidden * math.sqrt(0.5))
            bell = jnp.exp2(hidden * hidden * (-0.5 * math.log2(math.e))) * (1.0 / math.sqrt(2.0 * math.pi))
            r.act[rows, cols] = (hidden * cdf).astype(BF16)
            r.gh[rows, cols] = (grad_active * (cdf + hidden * bell)).astype(BF16)
        r.result[...] = (middle + dot(r.down_t[...], r.act[:, cols])).T
        grad_normed = dot(r.w_up[...], r.gh[:, cols])
        grad = cot.astype(F32) + norm_rows_back(grad_normed, gain, normed, inverse)
        r.grad[...] = grad
        r.ga_f[:, cols] = grad.astype(BF16)
        r.ln[0] += fold(grad_normed * normed)
        r.ln[1] += fold(grad_normed)

        @pl.when(i == steps - 1)
        def _():
            big = 512

            def one(j, _):
                rows = pl.ds(pl.multiple_of(j * big, big), big)
                r.d_up[:, rows] = dot_nt(r.low_f[...], r.gh[rows, :]).astype(BF16)
                r.d_down[rows, :] = dot_nt(r.act[rows, :], r.cot_f[...]).astype(BF16)
                return 0
            lax.fori_loop(0, ff // big, one, 0)
            r.d_up[:, ff:] = dot_nt(r.mixed[...], r.ga_f[...]).astype(BF16)

    return call.run(kernel, "feed_forward", (steps,))


def heads_backward(r, feat, cols):
    head = feat // HEADS
    scale = 1.0 / math.sqrt(head)
    rows = [pl.ds(h * head, head) for h in range(HEADS)]
    krows = [pl.ds(feat + h * head, head) for h in range(HEADS)]
    vrows = [pl.ds(2 * feat + h * head, head) for h in range(HEADS)]
    for h in range(HEADS):
        scaled = r.grad_mixed[rows[h], :] * r.inv[0, h:h + 1, :]
        r.lean[h:h + 1, :] = jnp.sum(scaled * r.mixed[rows[h], :].astype(F32), axis=0, keepdims=True)
        r.scaled[rows[h], :] = scaled.astype(BF16)
    for h in range(HEADS):
        r.scores[h] = dot(r.project[vrows[h], :].T, r.scaled[rows[h], :])
    for h in range(HEADS):
        r.grad_scores[h] = (r.powers[0, h].astype(F32) * (r.scores[h] - r.lean[h:h + 1, :])).astype(BF16)
    for h in range(HEADS):
        r.gp_f[vrows[h], cols] = dot_nt(r.scaled[rows[h], :], r.powers[0, h]).astype(BF16)
        r.gp_f[rows[h], cols] = (dot(r.project[krows[h], :], r.grad_scores[h]) * scale).astype(BF16)
        r.gp_f[krows[h], cols] = (dot_nt(r.project[rows[h], :], r.grad_scores[h]) * scale).astype(BF16)


def attention_backward(nz, chars, tokens, waves, small, w_qkv, w_out, saved, ff):
    feat, n = saved["start"].shape
    seqs = saved["powers"].shape[0]
    length = n // seqs
    call = Call()
    late = lambda i: jnp.maximum(i - seqs, 0)
    soon = lambda i: jnp.minimum(i, seqs - 1)
    call.arg("tok", tokens.reshape(seqs, 1, length), pl.BlockSpec((1, 1, length), lambda i: (late(i), 0, 0)))
    call.arg("waves", waves, whole(waves.shape))
    call.arg("small", small, whole((feat, 128)))
    call.arg("w_qkv", w_qkv, whole(w_qkv.shape))
    call.arg("w_out", w_out, whole(w_out.shape))
    call.arg("start", saved["start"], pl.BlockSpec((feat, length), lambda i: (0, i % seqs)))
    call.arg("grad", saved["grad"], pl.BlockSpec((feat, length), lambda i: (0, i % seqs)))
    for name, rows in (("project", 3 * feat), ("mixed", feat)):
        call.arg(name, saved[name], pl.BlockSpec((rows, length), lambda i: (0, soon(i))))
    call.arg("powers", saved["powers"], pl.BlockSpec((1, HEADS, length, length), lambda i: (soon(i), 0, 0, 0)))
    call.arg("inv", saved["inv"], pl.BlockSpec((1, HEADS, length), lambda i: (soon(i), 0, 0)))
    call.arg("ln2", saved["ln"], whole((2, feat, 128)))
    call.out("d_in", (feat, n), F32, pl.BlockSpec((feat, length), lambda i: (0, late(i))))
    call.temp("ln1", pltpu.VMEM((2, feat, 128), F32))
    call.temp("d_char", pltpu.VMEM((feat, 128), F32))
    call.temp("low_f", pltpu.VMEM((feat, n), BF16))
    call.temp("gp_f", pltpu.VMEM((3 * feat, n), BF16))
    call.temp("scores", pltpu.VMEM((HEADS, length, length), F32))
    call.temp("grad_scores", pltpu.VMEM((HEADS, length, length), BF16))
    call.temp("grad_mixed", pltpu.VMEM((feat, length), F32))
    call.temp("scaled", pltpu.VMEM((feat, length), BF16))
    call.temp("lean", pltpu.VMEM((HEADS, length), F32))
    call.temp("gs_f", pltpu.VMEM((feat, 128), F32))
    if nz:
        devices = nz * 8
        per, down_per = feat // devices, ff // devices
        blocks = (nz,) + BLOCKS
        call.arg("d_up", saved["d_up"].reshape(blocks + (per, ff + feat)), ANYWHERE)
        call.arg("d_down", saved["d_down"].reshape(blocks + (down_per, feat)), ANYWHERE)
        for name, shape in (("o_up", (per, ff)), ("o_out", (per, feat)), ("o_down", (down_per, feat)), ("o_qkv", (per, 3 * feat)),
                            ("o_time", (per, feat)), ("o_char", (chars, per)), ("o_ln", (4, per))):
            call.out(name, shape, F32, whole(shape))
        tails = {"up": (per, ff + feat), "down": (down_per, feat), "qkv": (per, 3 * feat), "rest": (per, 128 + feat)}
        for name, tail in tails.items():
            for part, kind in zip(("own", "far", "near", "line", "sems"), Scatter.scratch(nz, tail, BF16)):
                call.temp(f"{name}_{part}", kind)
        for name in ("up", "down"):
            call.temp(f"{name}_kept", pltpu.VMEM((nz, 2, 2) + tails[name], BF16))
        call.temp("kept_sems", pltpu.SemaphoreType.DMA((2,)))
        call.temp("d_qkv", pltpu.VMEM(blocks + (per, 3 * feat), BF16))
        call.temp("d_rest", pltpu.VMEM(blocks + (per, 128 + feat), BF16))
    else:
        call.out("d_qkv", (feat, 3 * feat), BF16, whole((feat, 3 * feat)))
        call.out("d_rest", (feat, 128 + feat), BF16, whole((feat, 128 + feat)))

    def kernel(r):
        i = pl.program_id(0)
        if nz:
            z, x, y, c = place()
            group = lambda name, mine, kept: Scatter(nz, mine, kept, *[getattr(r, f"{name}_{p}") for p in ("own", "far", "near", "line", "sems")])
            up = group("up", r.d_up, lambda k, a, b, cols: r.up_kept[k, a, b, :, cols])
            down = group("down", r.d_down, lambda k, a, b, cols: r.down_kept[k, a, b, :, cols])
            qkv = group("qkv", r.d_qkv, lambda k, a, b, cols: r.d_qkv[k, a, b, c, :, cols])
            rest = group("rest", r.d_rest, lambda k, a, b, cols: r.d_rest[k, a, b, c, :, cols])
            keep = [pltpu.make_async_copy(g.mine.at[pl.ds(0, nz), :, :, c], kept, r.kept_sems.at[k])
                    for k, (g, kept) in enumerate(((up, r.up_kept), (down, r.down_kept)))]

        @pl.when(i == 0)
        def _():
            if nz:
                greet(nz)
                for copy in keep:
                    copy.start()
            r.ln1[...] = jnp.zeros_like(r.ln1)
            r.d_char[...] = jnp.zeros_like(r.d_char)
            r.gs_f[...] = jnp.zeros_like(r.gs_f)

        @pl.when(i < seqs)
        def _():
            cols = pl.ds(pl.multiple_of(i * length, length), length)
            grad_low = r.grad[...].astype(BF16)
            r.grad_mixed[...] = dot(r.w_out[...], grad_low).astype(BF16).astype(F32)
            heads_backward(r, feat, cols)
            normed, _ = norm_rows(r.start[...])
            r.low_f[:, cols] = (normed * param(r.small, chars) + param(r.small, chars + 1)).astype(BF16)

        def at(step, *acts):
            @pl.when(i == step)
            def _():
                for act in acts:
                    act()

        if nz:
            at(0, lambda: greeted(nz), up.cores, down.cores, lambda: [copy.wait() for copy in keep])
            at(1, up.corners)
            at(2, down.corners)
            at(4, up.sides)
            at(5, down.sides)
            at(seqs - 1, up.lines)
            at(seqs + 1, qkv.corners)
            at(seqs + 2, down.lines)
            at(seqs + 4, qkv.sides)
            at(seqs + 6, qkv.lines)

        tall = lambda value: value.astype(BF16).reshape(r.d_qkv.shape[:-1] + (value.shape[-1],))

        @pl.when(i == seqs)
        def _():
            for p in range(3):
                rows = pl.ds(p * feat, feat)
                r.d_qkv[..., rows] = tall(dot_nt(r.low_f[...], r.gp_f[rows, :]))
            if nz:
                qkv.cores()

        @pl.when(i >= seqs)
        def _():
            k = i - seqs
            cols = pl.ds(pl.multiple_of(k * length, length), length)
            normed, inverse = norm_rows(r.start[...])
            gain = param(r.small, chars)
            grad_normed = dot(r.w_qkv[...], r.gp_f[:, cols])
            d_in = r.grad[...] + norm_rows_back(grad_normed, gain, normed, inverse)
            r.d_in[...] = d_in
            r.ln1[0] += fold(grad_normed * normed)
            r.ln1[1] += fold(grad_normed)
            lane = lax.broadcasted_iota(jnp.int32, r.gs_f.shape, 1)
            r.gs_f[...] += jnp.where(lane == k, jnp.sum(d_in, axis=1, keepdims=True), 0.0)
            one_hot = (lax.broadcasted_iota(jnp.int32, (128, length), 0) == r.tok[0]).astype(BF16)
            high = d_in.astype(BF16)
            low = (d_in - high.astype(F32)).astype(BF16)
            r.d_char[...] += dot_nt(high, one_hot) + dot_nt(low, one_hot)

        @pl.when(i == 2 * seqs - 1)
        def _():
            lane = lax.broadcasted_iota(jnp.int32, r.d_char.shape, 1)
            small = jnp.where(lane < chars, r.d_char[...], 0.0)
            for k, ref in enumerate((r.ln1.at[0], r.ln1.at[1], r.ln2.at[0], r.ln2.at[1])):
                small = jnp.where(lane == chars + k, jnp.sum(ref[...], axis=1, keepdims=True), small)
            r.d_rest[..., :128] = tall(small)
            r.d_rest[..., 128:] = tall(dot_nt(r.waves[...], r.gs_f[...].astype(BF16)))
            if nz:
                rest.cores()
                total = up.total()
                r.o_up[...] = total[:, :ff]
                r.o_out[...] = total[:, ff:]
                r.o_down[...] = down.total()
                rest.corners()
                rest.sides()
                rest.lines()
                r.o_qkv[...] = qkv.total()
                total = rest.total()
                r.o_time[...] = total[:, 128:]
                turned = total[:, :128].T
                r.o_char[...] = turned[:chars]
                r.o_ln[...] = turned[chars:chars + 4]

    return call.run(kernel, "attention_backward", (2 * seqs,), 1 if nz else None)


def hand_over(d_in, parts, width=512):
    feat, n = d_in.shape
    call = Call()
    call.arg("d_in", d_in, lanes(feat, width))
    call.out("o_d_in", (n, feat), F32, pl.BlockSpec((width, feat), lambda i: (i, 0)))
    for name, part in parts.items():
        call.arg(name, part, whole(part.shape))
        if name == "ln":
            for k in range(part.shape[0]):
                call.out(f"o_ln{k}", (1, part.shape[1]), F32, whole((1, part.shape[1])))
        else:
            call.out("o_" + name, part.shape, F32, whole(part.shape))

    def kernel(r):
        r.o_d_in[...] = r.d_in[...].T

        @pl.when(pl.program_id(0) == 0)
        def _():
            for name in parts:
                if name == "ln":
                    for k in range(r.ln.shape[0]):
                        getattr(r, f"o_ln{k}")[...] = r.ln[k:k + 1]
                else:
                    getattr(r, "o_" + name)[...] = getattr(r, name)[...]

    return call.run(kernel, "hand_over", (n // width,))

AXES = ("gx", "gy")


def make_body(gx, gy):
    def gathered(*shards):
        return [lax.all_gather(s, AXES, axis=0, tiled=True) for s in shards]

    def summed(part):
        return lax.psum_scatter(part.astype(F32), AXES, scatter_dimension=0, tiled=True)

    def body(tokens, timesteps, cotangent, char_table, time_weight, ln1_gain, ln1_bias, w_qkv, w_attn_out, ln2_gain, ln2_bias, w_up, w_down):
        devices = gx * gy
        feat = time_weight.shape[1]
        ff = w_up.shape[1]
        chars = char_table.shape[0]
        per = feat // devices
        nz = gx // 2 if gy == 4 and gx % 2 == 0 and per % 16 == 0 and per <= 128 else 0
        shards = [char_table, ln1_gain, ln1_bias, ln2_gain, ln2_bias, time_weight, w_qkv, w_attn_out, w_up, w_down]
        if nz:
            saved = attention_forward(nz, tokens, timesteps, shards)
            small = saved["first_o"].reshape(feat, 128 + feat)
            w_qkv, w_attn_out, w_up, w_down = (saved[k].reshape(-1, saved[k].shape[-1]) for k in ("qkv_o", "out_o", "up", "down"))
        else:
            shards = [lax.all_gather(char_table, AXES, axis=1, tiled=True)] + gathered(*shards[1:])
            _, _, _, _, _, _, w_qkv, w_attn_out, w_up, w_down = shards
            saved = attention_forward(0, tokens, timesteps, shards)
            small = saved["small"]
        saved.update(feed_forward(chars, saved["middle"], cotangent, saved["mixed"], small, w_up, w_down))
        got = attention_backward(nz, chars, tokens, saved["waves"], small, w_qkv, w_attn_out, saved, ff)
        if nz:
            parts = {k: got["o_" + k] for k in ("up", "out", "down", "qkv", "time", "char", "ln")}
        else:
            up_out, down, qkv, rest = (summed(p) for p in (saved["d_up"], saved["d_down"], got["d_qkv"], got["d_rest"]))
            parts = {"up": up_out[:, :ff], "out": up_out[:, ff:], "down": down, "qkv": qkv, "time": rest[:, 128:],
                     "char": rest[:, :chars].T, "ln": rest[:, chars:chars + 4].T}
        o = hand_over(got["d_in"], parts)
        ln = [o[f"o_ln{k}"].reshape(per) for k in range(4)]
        return (saved["result"], o["o_d_in"], o["o_char"], o["o_time"], ln[0], ln[1], o["o_qkv"], o["o_out"], ln[2], ln[3], o["o_up"], o["o_down"])
    return body


def solution(mesh):
    every = P(AXES)
    rows, cols = P(AXES, None), P(None, AXES)
    return jax.shard_map(
        make_body(mesh.shape["gx"], mesh.shape["gy"]),
        mesh=mesh,
        in_specs=(every, every, rows, cols, rows, every, every, rows, rows, every, every, rows, rows),
        out_specs=(rows, rows, cols, rows, every, every, rows, rows, every, every, rows, rows),
        check_vma=False,
    )
```

time: 1230 us -> 169 us (0.14)
  waiting for transfers between devices: 699 us -> 0 us
  blocking collectives: 200 us -> 0 us
  matrix products: 199 us -> 0 us
  Pallas kernels: 0 us -> 165 us
  local copies, waits for them, and re-layouts: 79.2 us -> 2.76 us
  other arithmetic: 30.9 us -> 0 us
  between operations: 14.9 us -> 0.67 us
    reduce_scatter x6 -> x0, waiting for transfers between devices: 697 us -> none  [the longest x1 143 us: body(): lax.psum_scatter(ffn_grads[2], ('gx', 'gy'), scatter_dimension=0, tiled=T...]
    dot_general x23 -> x0, matrix products: 199 us -> none  [the longest x1 44.2 us: ffn_parts(): hidden = jnp.dot(normed_low, up_weight, preferred_element_type=jnp.float32)]
    pallas_call x0 -> x4, Pallas kernels: none -> 165 us  [run(): pl.pallas_call(body, grid=grid, in_specs=[s for *_, s in self.ins], out_s...]
    all_gather x3 -> x0, blocking collectives: 126 us -> none  [the longest x1 45 us: body(): lax.all_gather(time_weight, ('gx', 'gy'), axis=0, tiled=True)]
    unnamed x2 -> x0, blocking collectives: 74.4 us -> none
    unnamed x102 -> x2, local copies, waits for them, and re-layouts: 34.5 us -> 2.76 us
    reshape x3 -> x0, local copies, waits for them, and re-layouts: 25.1 us -> none  [the longest x1 16.3 us: attention_parts(): project.reshape(seq_count, start.shape[0] // seq_count, 3, HEADS, head_size)]
    convert_element_type x6 -> x0, other arithmetic: 13.1 us -> none  [the longest x1 12.4 us: attention_backward(): grad_scores = (probabilities * (grad_probs - jnp.sum(grad_probs * probabi...]
  transfers between devices with their start and end apart: 9 -> 0, of which waited for: 6 -> 0; matrix products, arithmetic and copies ran while one was open for 16% -> 0% of each run, Pallas kernels for 0% -> 0%
where the time goes in v2:
time: 169 us; the launch traced here: 168 us
  Pallas kernels  165 us (98%)
  local copies, waits for them, and re-layouts  2.76 us (2%)
    pallas_call x4, Pallas kernels, run(): pl.pallas_call(body, grid=grid, in_specs=[s for *_, s in self.ins], out_s...  165 us

profile of v2, /device:TPU:0, one launch (start us, length us, event | category | flops | bytes accessed | tf_op | source)
XLA Modules:
  0.0 168.2 jit_solution(15576328287697045335)
XLA Ops:
  0.6 1.4 copy.25.refs_2_
  2.0 56.2 %attention_forward.1 = (f32[512,2048]{1,0:T(8,128)}, f32[512,2048]{1,0:T(8,128)}, bf16[1536,2048]{1,0:T(8,128)(2,1)}, bf16[512,2048]{1,0:T(8,128)(2,1)}, bf16[8,...) custom-call(s32[8,1,256]{2,1,0:T(1,128)} %bitcast.25, ...), custom_call_target="tpu_custom_call" | custom-call | tf_op jit(solution)/shard_map/attention_forward/pallas_call | solution.py:256
  58.2 43.0 %feed_forward.1 = (f32[2048,512]{1,0:T(8,128)}, f32[512,2048]{1,0:T(8,128)}, f32[2,512,128]{2,1,0:T(8,128)}, bf16[512,2560]{1,0:T(8,128)(2,1)}, bf16[2048,512]{1,0:T(8,128)(2,1)}) custom-call(f32[512,2048]{1,0:T(8,128)} %get-tuple-element.48.refs_0_, bf16[2048,512]{1,0:T(8,128)(2,1)} %refs_1_.1, bf16[512,2048]{1,0:T(8,128)(2,1)} %get-tuple-element.49.refs_2_.refs_8_, ...), custom_call_target="tpu_custom_call" | custom-call | tf_op jit(solution)/shard_map/feed_forward/pallas_call | solution.py:256
  101.3 60.0 %attention_backward.1 = (f32[512,2048]{1,0:T(8,128)}, f32[16,2048]{1,0:T(8,128)}, f32[16,512]{1,0:T(8,128)}, f32[64,512]{1,0:T(8,128)}, f32[16,1536]{1,0:T(8,128...) custom-call(s32[8,1,256]{2,1,0:T(1,128)} %bitcast.26, bf16[512,128]{1,0:T(8,128)(2,1)} %get-tuple-element.54.refs_1_, ...), custom_call_target="tpu_custom_call" | custom-call | tf_op jit(solution)/shard_map/attention_backward/pallas_call | solution.py:256
  161.3 5.6 %hand_over.1 = (f32[2048,512]{1,0:T(8,128)}, f32[16,2048]{1,0:T(8,128)}, f32[16,512]{1,0:T(8,128)}, f32[64,512]{1,0:T(8,128)}, f32[16,1536]{1,0:T(8,128)}, /*ind...) custom-call(f32[512,2048]{1,0:T(8,128)} %get-tuple-element.65.refs_0, ...), custom_call_target="tpu_custom_call" | custom-call | tf_op jit(solution)/shard_map/hand_over/pallas_call | solution.py:256
  166.8 1.4 copy.26

commit v3 on v0

v3 whole, which is shorter than its diff:
```python
import math
import types

import jax
import jax.numpy as jnp
from jax import lax
from jax.experimental import pallas as pl
from jax.experimental.pallas import tpu as pltpu
from jax.sharding import PartitionSpec as P

F32, BF16 = jnp.float32, jnp.bfloat16
MESH = pl.DeviceIdType.MESH
AXES = ("gx", "gy")
HEADS = 8
EPSILON = 1e-05
VMEM_LIMIT = 63 * 2**20
BLOCKS = (2, 2, 2)
X, Y, CORE = range(3)


def place():
    gx, gy = lax.axis_index(AXES[0]), lax.axis_index(AXES[1])
    return gx // 2, gx % 2, gy // 2, gy % 2


def device(z, x, y, c):
    return (z * 2 + x, y * 2 + c)


def across(axis):
    z, x, y, c = place()
    return ((z, 1 - x, y, c), (z, x, 1 - y, c), (z, x, y, 1 - c))[axis]


def greet(nz):
    z, x, y, c = place()
    barrier = pltpu.get_barrier_semaphore()
    for where in [across(axis) for axis in (X, Y, CORE)] + [((z + d) % nz, x, y, c) for d in range(1, nz)]:
        pl.semaphore_signal(barrier, inc=1, device_id=device(*where), device_id_type=MESH)


def greeted(nz):
    pl.semaphore_wait(pltpu.get_barrier_semaphore(), 3 + nz - 1)


def halves(width):
    middle = width // 256 * 128
    return pl.ds(0, middle), pl.ds(middle, width - middle)


def blocks_of(out, number):
    if number % 4:
        return out.at[pl.ds(0, number), 0, 0, 0]
    return out.at[pl.ds(0, number // 4), :, :, 0]


class Gather:
    LINES, SIDES, CORNERS, CORES = range(4)

    @staticmethod
    def scratch(nz):
        return pltpu.SemaphoreType.DMA((2, 4))

    def __init__(self, nz, shard, out, sems):
        self.nz, self.shard, self.out, self.sems = nz, shard, out, sems
        self.zs, self.count, self.base, self.waits = pl.ds(0, nz), nz, 0, True

    def send(self, src, dst, sent, came, where):
        return pltpu.make_async_remote_copy(
            src_ref=src, dst_ref=dst, send_sem=self.sems.at[0, sent + (self.base if sent else 0)],
            recv_sem=self.sems.at[1, came + (self.base if came else 0)], device_id=device(*where), device_id_type=MESH)

    def some(self, number, stage):
        ref = blocks_of(self.out, number)
        return self.send(ref, ref, stage, stage, across(CORE))

    def pass_on(self, axis, a, b, sent, came, cut=None):
        c = place()[3]
        ref = self.out.at[self.zs, a, b, c]
        if cut is not None:
            ref = ref.at[:, :, cut]
        self.send(ref, ref, sent, came, across(axis)).start()

    def lines(self):
        z, x, y, c = place()
        for d in range(1, self.nz):
            self.send(self.shard, self.out.at[z, x, y, c], self.LINES, self.LINES, ((z + d) % self.nz, x, y, c)).start()

    def arrived(self):
        self.some(self.nz - 1, self.LINES).wait_recv()

    def sides(self):
        _, x, y, _ = place()
        if self.waits:
            self.arrived()
        self.pass_on(X, x, y, self.SIDES, self.SIDES)
        self.pass_on(Y, x, y, self.SIDES, self.SIDES)
        self.pass_on(CORE, x, y, self.SIDES, self.CORES)

    def corners(self):
        _, x, y, _ = place()
        lo, hi = halves(self.out.shape[-1])
        self.some(2 * self.count, self.SIDES).wait_recv()
        self.pass_on(X, x, 1 - y, self.CORNERS, self.CORNERS, lo)
        self.pass_on(Y, 1 - x, y, self.CORNERS, self.CORNERS, hi)
        self.pass_on(CORE, 1 - x, y, self.CORNERS, self.CORES)
        self.pass_on(CORE, x, 1 - y, self.CORNERS, self.CORES)

    def cores(self):
        _, x, y, _ = place()
        self.some(self.count, self.CORNERS).wait_recv()
        self.pass_on(CORE, 1 - x, 1 - y, self.CORES, self.CORES)

    def whole(self):
        self.some(4 * self.count, self.CORES).wait_recv()

    def sent(self):
        self.some(3 * self.count, self.SIDES).wait_send()
        self.some(3 * self.count, self.CORNERS).wait_send()
        self.some(self.count, self.CORES).wait_send()

    def finish(self):
        self.some(self.nz - 1, self.LINES).wait_send()
        self.sent()


class GatherLayers(Gather):
    @staticmethod
    def scratch(nz):
        return pltpu.SemaphoreType.DMA((2, 1 + 3 * nz))

    def layer(self, j):
        one = Gather(self.nz, self.shard, self.out, self.sems)
        one.zs, one.count, one.base, one.waits = pl.ds(j, 1), 1, 3 * j, False
        return one

    def sent(self):
        for j in range(self.nz):
            self.layer(j).sent()


class Scatter:
    @staticmethod
    def scratch(nz, tail):
        return [pltpu.VMEM((nz, 2, 2) + tail, BF16), pltpu.VMEM((nz,) + tail, BF16), pltpu.VMEM((2, nz) + tail, BF16),
                pltpu.VMEM((nz - 1,) + tail, BF16), pltpu.SemaphoreType.DMA((2, 4))]

    def __init__(self, nz, mine, temps, kept=None):
        self.nz, self.mine, self.kept = nz, mine, kept
        self.own, self.far, self.near, self.line, self.sems = temps
        self.width = self.own.shape[-1]

    def send(self, src, dst, stage, where):
        return pltpu.make_async_remote_copy(
            src_ref=src, dst_ref=dst, send_sem=self.sems.at[0, stage], recv_sem=self.sems.at[1, stage],
            device_id=device(*where), device_id_type=MESH)

    def done(self, ref, stage):
        self.send(ref, ref, stage, across(CORE)).wait()

    def add(self, a, b, cols, *values):
        spot = (slice(None), a, b, slice(None), cols)
        total = self.own[spot]
        for value in values:
            total = total + value
        self.own[spot] = total

    def cores(self):
        c = place()[3]
        self.send(self.mine.at[pl.ds(0, self.nz), :, :, 1 - c], self.own, 0, across(CORE)).start()

    def corners(self):
        _, x, y, c = place()
        every, all_z = pl.ds(0, self.width), pl.ds(0, self.nz)
        lo, hi = halves(self.width)
        self.done(self.own, 0)
        for number, (a, b) in enumerate(((1 - x, 1 - y), (1 - x, y), (x, 1 - y), (x, y))):
            self.add(a, b, every, self.mine[:, a, b, c] if self.kept is None else self.kept[:, a, b])
            if number == 0:
                self.send(self.own.at[all_z, 1 - x, 1 - y, :, lo], self.far.at[:, :, lo], 1, across(X)).start()
                self.send(self.own.at[all_z, 1 - x, 1 - y, :, hi], self.far.at[:, :, hi], 1, across(Y)).start()

    def sides(self):
        _, x, y, _ = place()
        all_z = pl.ds(0, self.nz)
        lo, hi = halves(self.width)
        self.done(self.far, 1)
        self.add(x, 1 - y, lo, self.far[:, :, lo])
        self.send(self.own.at[all_z, x, 1 - y], self.near.at[1], 2, across(Y)).start()
        self.add(1 - x, y, hi, self.far[:, :, hi])
        self.send(self.own.at[all_z, 1 - x, y], self.near.at[0], 2, across(X)).start()

    def lines(self):
        z, x, y, c = place()
        self.done(self.near, 2)
        self.add(x, y, pl.ds(0, self.width), self.near[0], self.near[1])
        for d in range(1, self.nz):
            to = (z + d) % self.nz
            self.send(self.own.at[to, x, y], self.line.at[d - 1], 3, (to, x, y, c)).start()

    def total(self):
        z, x, y, _ = place()
        self.done(self.line, 3)
        total = self.own[z, x, y].astype(F32)
        for d in range(1, self.nz):
            total = total + self.line[d - 1].astype(F32)
        return total


class Call:
    def __init__(self):
        self.ins, self.outs, self.temps = {}, {}, {}

    def arg(self, **named):
        self.ins.update(named)

    def out(self, **named):
        self.outs.update(named)

    def temp(self, **named):
        self.temps.update(named)

    def run(self, kernel, name, steps, collective=None):
        kinds = [k for kind in self.temps.values() for k in (kind if isinstance(kind, list) else [kind])]

        def body(*refs):
            refs = iter(refs)
            r = types.SimpleNamespace(**{n: next(refs) for n in [*self.ins, *self.outs]})
            for n, kind in self.temps.items():
                setattr(r, n, [next(refs) for _ in kind] if isinstance(kind, list) else next(refs))
            kernel(r)
        extra = {} if collective is None else dict(collective_id=collective, has_side_effects=True)
        got = pl.pallas_call(
            body, grid=(steps,), in_specs=[spec for _, spec in self.ins.values()], out_specs=[spec for *_, spec in self.outs.values()],
            out_shape=[jax.ShapeDtypeStruct(shape, kind) for shape, kind, _ in self.outs.values()], scratch_shapes=kinds,
            compiler_params=pltpu.CompilerParams(vmem_limit_bytes=VMEM_LIMIT, **extra), name=name,
        )(*[array for array, _ in self.ins.values()])
        return types.SimpleNamespace(**dict(zip(self.outs, got)))


def whole(shape):
    return pl.BlockSpec(tuple(shape), lambda i: (0,) * len(shape))


def lanes(rows, width, at=lambda i: i):
    return pl.BlockSpec((rows, width), lambda i: (0, at(i)))


ANYWHERE = pl.BlockSpec(memory_space=pl.ANY)


def dispatch(i, table):
    steps = sorted(table)

    def among(some):
        if len(some) == 1:
            @pl.when(i == some[0])
            def _():
                for act in table[some[0]]:
                    act()
            return
        half = len(some) // 2
        pl.when(i < some[half])(lambda: among(some[:half]))
        pl.when(i >= some[half])(lambda: among(some[half:]))
    if steps:
        among(steps)


def dot(left, right):
    return jnp.dot(left, right, preferred_element_type=F32)


def dot_nt(left, right):
    return lax.dot_general(left, right, (((1,), (1,)), ((), ())), preferred_element_type=F32)


def norm_rows(values):
    count = values.shape[0]
    shifted = values - jnp.sum(values, axis=0, keepdims=True) * (1.0 / count)
    inverse = lax.rsqrt(jnp.sum(shifted * shifted, axis=0, keepdims=True) * (1.0 / count) + EPSILON)
    return shifted * inverse, inverse


def norm_rows_back(grad, gain, normed, inverse):
    count = grad.shape[0]
    scaled = grad * gain
    lean = jnp.sum(scaled, axis=0, keepdims=True) * (1.0 / count)
    turn = jnp.sum(scaled * normed, axis=0, keepdims=True) * (1.0 / count)
    return inverse * (scaled - lean - normed * turn)


def fold(values):
    total = values[:, :128]
    for k in range(1, values.shape[1] // 128):
        total = total + values[:, 128 * k:128 * (k + 1)]
    return total


def flat(ref, cols=slice(None)):
    value = ref[(slice(None),) * (len(ref.shape) - 1) + (cols,)]
    return value.reshape(-1, value.shape[-1])


def param(table, column):
    return table[:, column:column + 1].astype(F32)


def gelu_parts(hidden, grad_active):
    cdf = 0.5 + 0.5 * lax.erf(hidden * math.sqrt(0.5))
    bell = jnp.exp2(hidden * hidden * (-0.5 * math.log2(math.e))) * (1.0 / math.sqrt(2.0 * math.pi))
    return (hidden * cdf).astype(BF16), (grad_active.astype(BF16).astype(F32) * (cdf + hidden * bell)).astype(BF16)


def fill_waves(r, feat):
    half = feat // 2
    r.steps_row[...] = jnp.zeros_like(r.steps_row)
    r.steps_row[:, :r.steps.shape[1]] = r.steps[...].astype(F32)
    rate = jnp.exp(lax.broadcasted_iota(jnp.int32, (half, 128), 0).astype(F32) * (-math.log(10000.0) / half))
    angles = rate * r.steps_row[...]
    r.waves[:half, :] = jnp.sin(angles).astype(BF16)
    r.waves[half:, :] = jnp.cos(angles).astype(BF16)


def fill_small(r, chars):
    count = r.char.shape[0]
    r.square[...] = jnp.zeros_like(r.square)
    for k, ref in enumerate((r.g1, r.b1, r.g2, r.b2)):
        r.square[chars + k:chars + k + 1, :count] = ref[...].astype(F32)
    r.small_shard[...] = r.square[...].T[:count].astype(BF16)
    r.small_shard[:, :chars] = r.char[...]


def one_hot_of(tok):
    return (lax.broadcasted_iota(jnp.int32, (128, tok.shape[1]), 0) == tok).astype(BF16)


class Heads:
    def __init__(self, feat):
        self.size = feat // HEADS
        self.q, self.k, self.v = ([pl.ds(part * feat + h * self.size, self.size) for h in range(HEADS)] for part in range(3))

    def scores(self, project, scores):
        for h in range(HEADS):
            scores[h] = dot(project[self.k[h], :].T, project[self.q[h], :])

    def softmax(self, scores, powers, inverses):
        turn = math.log2(math.e) / math.sqrt(self.size)
        for h in range(HEADS):
            value = scores[h]
            power = jnp.exp2((value - jnp.max(value, axis=0, keepdims=True)) * turn)
            inverses[h:h + 1, :] = 1.0 / jnp.sum(power, axis=0, keepdims=True)
            powers[h] = power.astype(BF16)

    def mix(self, project, powers, inverses, mixed):
        for h in range(HEADS):
            mixed[self.q[h], :] = (dot(project[self.v[h], :], powers[h]) * inverses[h:h + 1, :]).astype(BF16)

    def scale_grad(self, grad_mixed, inverses, mixed, scaled, lean):
        for h in range(HEADS):
            value = grad_mixed[self.q[h], :] * inverses[h:h + 1, :]
            lean[h:h + 1, :] = jnp.sum(value * mixed[self.q[h], :].astype(F32), axis=0, keepdims=True)
            scaled[self.q[h], :] = value.astype(BF16)

    def grad_probs(self, project, scaled, scores):
        for h in range(HEADS):
            scores[h] = dot(project[self.v[h], :].T, scaled[self.q[h], :])

    def grad_scores(self, powers, scores, lean, grads):
        for h in range(HEADS):
            grads[h] = (powers[h].astype(F32) * (scores[h] - lean[h:h + 1, :])).astype(BF16)

    def grad_project(self, project, scaled, powers, grads, out, cols):
        scale = 1.0 / math.sqrt(self.size)
        for h in range(HEADS):
            out[self.v[h], cols] = dot_nt(scaled[self.q[h], :], powers[h]).astype(BF16)
            out[self.q[h], cols] = (dot(project[self.k[h], :], grads[h]) * scale).astype(BF16)
            out[self.k[h], cols] = (dot_nt(project[self.q[h], :], grads[h]) * scale).astype(BF16)


def forward(nz, tokens, timesteps, cotangent, char, g1, b1, g2, b2, time_w, w_qkv, w_out, w_up, w_down, chunk=512):
    seqs = timesteps.shape[0]
    n = tokens.shape[0]
    length = n // seqs
    feat, ff = time_w.shape[1], w_up.shape[1]
    count, chars = char.shape
    pair = 2 if seqs % 2 == 0 else 1
    items, width = seqs // pair, pair * length
    wide = ff // nz if nz else 512
    tiles, chunks = ff // wide, n // chunk
    item_of = lambda i: jnp.minimum(i, items - 1)
    tile_of = lambda i: jnp.clip(i - items, 0, tiles - 1)
    chunk_of = lambda i: jnp.maximum(i - items - tiles, 0)
    heads = Heads(feat)
    call = Call()
    at_once = lambda value: (value, whole(value.shape))
    call.arg(tok=at_once(tokens.reshape(seqs, 1, length)), steps=at_once(timesteps.reshape(1, seqs)), char=at_once(char),
             g1=at_once(g1.reshape(1, count)), b1=at_once(b1.reshape(1, count)), g2=at_once(g2.reshape(1, count)),
             b2=at_once(b2.reshape(1, count)), time_w=at_once(time_w), w_qkv=at_once(w_qkv), w_out=at_once(w_out), w_up=at_once(w_up),
             w_down=at_once(w_down), cot=(cotangent, pl.BlockSpec((width, feat), lambda i: (item_of(i), 0))))
    call.out(start_o=((feat, n), F32, ANYWHERE), mixed_o=((feat, n), BF16, ANYWHERE), project_o=((3 * feat, n), BF16, ANYWHERE),
             powers=((seqs, HEADS, length, length), BF16, pl.BlockSpec((pair, HEADS, length, length), lambda i: (item_of(i), 0, 0, 0))),
             inv=((seqs, HEADS, length), F32, whole((seqs, HEADS, length))), waves=((feat, 128), BF16, whole((feat, 128))),
             grad=((feat, n), F32, lanes(feat, chunk, chunk_of)), ln=((2, feat, 128), F32, whole((2, feat, 128))),
             d_down=((ff, feat), BF16, pl.BlockSpec((ff // chunks, feat), lambda i: (chunk_of(i), 0))),
             middle_o=((feat, n), F32, ANYWHERE), act_o=((ff, n), BF16, ANYWHERE), down_o=((feat, ff), BF16, ANYWHERE))
    parts = 3
    if nz:
        per = feat // (nz * 8)
        blocks = lambda tail: (nz,) + BLOCKS + tail
        landing = lambda *tail: pltpu.VMEM(blocks(tail), BF16)
        sems = Gather.scratch(nz)
        call.temp(first=landing(count, 128 + feat), first_sems=sems, out=landing(count, feat), out_sems=sems,
                  qkv=[landing(count, feat)] * parts, qkv_sems=[sems] * parts, ups=[landing(count, wide)] * tiles, up_sems=[sems] * tiles,
                  down=landing(*w_down.shape), down_sems=GatherLayers.scratch(nz), first_shard=pltpu.VMEM((count, 128 + feat), BF16),
                  save_sems=pltpu.SemaphoreType.DMA((2 + parts,)),
                  mine=pltpu.VMEM((tiles,) + blocks((per, wide)), BF16), sums=Scatter.scratch(nz, (per, wide)) * tiles)
        call.out(first_o=(blocks((count, 128 + feat)), BF16, ANYWHERE), out_o=(blocks((count, feat)), BF16, ANYWHERE),
                 qkv_o=(blocks(w_qkv.shape), BF16, ANYWHERE), o_up=((per, ff), F32, whole((per, ff))))
    else:
        call.out(small=((count, 128), BF16, whole((count, 128))), d_up=((feat, ff), BF16, lanes(feat, wide, tile_of)))
    vmem = lambda kind, *shape: pltpu.VMEM(shape, kind)
    call.temp(small_shard=vmem(BF16, count, 128), square=vmem(F32, 128, max(count, 128)), steps_row=vmem(F32, 1, 128),
              stamps=vmem(F32, feat, 128), out_t=vmem(BF16, feat, feat), starts=vmem(F32, feat, n), mixed=vmem(BF16, feat, n),
              scores=vmem(F32, pair * HEADS, length, length), middle=vmem(F32, feat, n), low2=vmem(BF16, feat, n), cot_f=vmem(BF16, feat, n),
              down_t=vmem(BF16, feat, ff), up=vmem(BF16, feat, ff), up_t=vmem(BF16, wide, feat), down_rows=vmem(BF16, wide, feat),
              act=vmem(BF16, ff, n), gh=vmem(BF16, ff, n), later_sems=pltpu.SemaphoreType.DMA((3,)), soon_sems=pltpu.SemaphoreType.DMA((3,)))

    def kernel(r):
        i = pl.program_id(0)
        proj, low = r.act.at[pl.ds(0, 3 * feat)], r.gh.at[pl.ds(0, feat)]
        later = [pltpu.make_async_copy(a, b, r.later_sems.at[k])
                 for k, (a, b) in enumerate(((r.middle, r.middle_o), (r.act, r.act_o), (r.down_t, r.down_o)))]
        soon = [pltpu.make_async_copy(a, b, r.soon_sems.at[k])
                for k, (a, b) in enumerate(((proj, r.project_o), (r.starts, r.start_o), (r.mixed, r.mixed_o)))]
        if nz:
            z, x, y, c = place()
            first = Gather(nz, r.first_shard, r.first, r.first_sems)
            qkv = [Gather(nz, r.w_qkv.at[:, pl.ds(p * feat, feat)], r.qkv[p], r.qkv_sems[p]) for p in range(parts)]
            out = Gather(nz, r.w_out, r.out, r.out_sems)
            ups = [Gather(nz, r.w_up.at[:, pl.ds(j * wide, wide)], r.ups[j], r.up_sems[j]) for j in range(tiles)]
            down = GatherLayers(nz, r.w_down, r.down, r.down_sems)
            needs = [(ups[j], down.layer(j)) for j in range(tiles)]
            every = (pl.ds(0, nz), slice(None), slice(None), slice(None), slice(None))
            save = [pltpu.make_async_copy(r.first, r.first_o, r.save_sems.at[0]), pltpu.make_async_copy(r.out, r.out_o, r.save_sems.at[1])]
            save += [pltpu.make_async_copy(g.out, r.qkv_o.at[every + (pl.ds(p * feat, feat),)], r.save_sems.at[2 + p]) for p, g in enumerate(qkv)]
            groups = [Scatter(nz, r.mine.at[j], r.sums[5 * j:5 * j + 5]) for j in range(tiles)]

        def small():
            return flat(r.first, slice(0, 128)) if nz else r.small[...]

        def begin(some):
            table = small()
            for k in some:
                cols = pl.ds(k * length, length)
                lane = lax.broadcasted_iota(jnp.int32, r.stamps.shape, 1)
                stamp = jnp.sum(jnp.where(lane == k, r.stamps[...], 0.0), axis=1, keepdims=True)
                start = dot(table, one_hot_of(r.tok[k])) + stamp
                r.starts[:, cols] = start
                normed, _ = norm_rows(start)
                low[:, cols] = (normed * param(table, chars) + param(table, chars + 1)).astype(BF16)

        def multiply(p, weights):
            proj[p * feat:(p + 1) * feat] = dot(weights.T, low[...]).astype(BF16)

        def prelude():
            r.ln[...] = jnp.zeros_like(r.ln)
            if not nz:
                fill_small(r, chars)
                r.small[...] = r.small_shard[...]
                fill_waves(r, feat)
                r.stamps[...] = dot(r.time_w[...].T, r.waves[...])
                r.out_t[...] = r.w_out[...].T
                begin(range(seqs))
                for p in range(parts):
                    multiply(p, r.w_qkv[:, p * feat:(p + 1) * feat])
                for copy in soon[:2]:
                    copy.start()
                return
            greet(nz)
            fill_small(r, chars)
            q, k, v = qkv
            r.first_shard[:, :128] = r.small_shard[...]
            r.first_shard[:, 128:] = r.time_w[...]
            for g in (first, out, q, k, v, *ups, down):
                g.out[z, x, y, c] = g.shard[...]
            greeted(nz)
            first.lines()
            q.lines()
            fill_waves(r, feat)
            first.sides()
            k.lines()
            q.sides()
            v.lines()
            first.corners()
            k.sides()
            out.lines()
            q.corners()
            first.cores()
            v.sides()
            ups[0].lines()
            k.corners()
            q.cores()
            first.whole()
            r.stamps[...] = dot(flat(r.first, slice(128, 128 + feat)).T, r.waves[...])
            begin(range(0, seqs // 2))
            out.sides()
            down.lines()
            v.corners()
            k.cores()
            begin(range(seqs // 2, seqs))
            soon[1].start()
            q.whole()
            multiply(0, flat(r.qkv[0]))
            out.corners()
            v.cores()
            ups[0].sides()
            ups[1].lines()
            k.whole()
            multiply(1, flat(r.qkv[1]))
            v.whole()
            multiply(2, flat(r.qkv[2]))
            soon[0].start()
            out.cores()
            for g in ups[2:]:
                g.lines()
            down.arrived()
            needs[0][1].sides()

        def all_out():
            if nz:
                out.whole()
                r.out_t[...] = flat(r.out).T
                for copy in save:
                    copy.start()

        def tile_weights(j):
            if nz:
                for part in needs[j]:
                    part.whole()
                tile = flat(r.ups[j])
                r.down_rows[...] = flat(r.down.at[pl.ds(j, 1)])
            else:
                tile = r.w_up[:, j * wide:(j + 1) * wide]
                r.down_rows[...] = r.w_down[j * wide:(j + 1) * wide]
            r.up[:, j * wide:(j + 1) * wide] = tile
            r.up_t[...] = tile.T

        before = {}

        def at(step, *acts):
            before.setdefault(step, []).extend(acts)

        at(0, prelude)
        if nz:
            for j, some in enumerate(needs):
                for part in some:
                    if j > 0:
                        at(j, part.sides)
                    at(j + 1, part.corners)
                    at(j + 2, part.cores)
            for j, g in enumerate(groups):
                at(items + j + 1, g.cores)
                at(items + j + 2, g.corners)
                at(items + j + 3, g.sides)
                at(items + j + 4, g.lines)
        at(items, *[copy.wait for copy in soon[:2]], soon[2].start)
        for j in range(tiles):
            at(items + j, lambda j=j: tile_weights(j))
        at(items + tiles, soon[2].wait, *[copy.start for copy in later])
        dispatch(i, before)

        @pl.when(i < items)
        def _():
            def views(k):
                cols = pl.ds(pl.multiple_of((i * pair + k) * length, length), length)
                return proj.at[:, cols], r.scores.at[pl.ds(k * HEADS, HEADS)], r.powers.at[k], r.inv.at[i * pair + k], r.mixed.at[:, cols]

            for k in range(pair):
                project, scores, powers, inverses, mixed = views(k)
                heads.scores(project, scores)
            for k in range(pair):
                project, scores, powers, inverses, mixed = views(k)
                heads.softmax(scores, powers, inverses)
                heads.mix(project, powers, inverses, mixed)
            pl.when(i == 0)(all_out)
            cols = pl.ds(pl.multiple_of(i * width, width), width)
            middle = r.starts[:, cols] + dot(r.out_t[...], r.mixed[:, cols])
            r.middle[:, cols] = middle
            normed, _ = norm_rows(middle)
            r.low2[:, cols] = (normed * param(small(), chars + 2) + param(small(), chars + 3)).astype(BF16)
            r.cot_f[:, cols] = r.cot[...].T

        @pl.when((i >= items) & (i < items + tiles))
        def _():
            first_row = pl.multiple_of((i - items) * wide, wide)
            rows = pl.ds(first_row, wide)
            r.down_t[:, rows] = r.down_rows[...].T
            for t in range(chunks):
                cols = pl.ds(t * chunk, chunk)
                for half in range(2):
                    some = pl.ds(half * wide // 2, wide // 2)
                    part = pl.ds(pl.multiple_of(first_row + half * (wide // 2), wide // 2), wide // 2)
                    r.act[part, cols], r.gh[part, cols] = gelu_parts(
                        dot(r.up_t[some, :], r.low2[:, cols]), dot(r.down_rows[some, :], r.cot_f[:, cols]))
            d_up = dot_nt(r.low2[...], r.gh[rows, :]).astype(BF16)
            if nz:
                r.mine[i - items] = d_up.reshape(blocks((per, wide)))
            else:
                r.d_up[...] = d_up

        @pl.when(i >= items + tiles)
        def _():
            cols = pl.ds(pl.multiple_of((i - items - tiles) * chunk, chunk), chunk)
            grad_normed = dot(r.up[...], r.gh[:, cols])
            share = ff // chunks
            r.d_down[...] = dot_nt(r.act[pl.ds(pl.multiple_of((i - items - tiles) * share, share), share), :], r.cot_f[...]).astype(BF16)
            normed, inverse = norm_rows(r.middle[:, cols])
            gain = param(small(), chars + 2)
            r.grad[...] = r.cot_f[:, cols].astype(F32) + norm_rows_back(grad_normed, gain, normed, inverse)
            r.ln[0] += fold(grad_normed * normed)
            r.ln[1] += fold(grad_normed)

        @pl.when(i == items + tiles + chunks - 1)
        def _():
            for copy in later:
                copy.wait()
            if nz:
                for g in (first, *qkv, out, *ups, down):
                    g.finish()
                for copy in save:
                    copy.wait()
                for j in range(tiles):
                    r.o_up[:, j * wide:(j + 1) * wide] = groups[j].total()

    return call.run(kernel, "forward_and_ffn", items + tiles + chunks, 0 if nz else None)


def backward(nz, chars, tokens, small, w_qkv, w_out, saved, chunk=512):
    feat, n = saved.start_o.shape
    seqs = saved.powers.shape[0]
    ff = saved.act_o.shape[0]
    length = n // seqs
    pair = 2 if seqs % 2 == 0 else 1
    items, width, chunks = seqs // pair, pair * length, n // chunk
    heads = Heads(feat)
    late = lambda i: jnp.clip(i - items, 0, items - 1)
    soon = lambda i: jnp.minimum(i, items - 1)
    twice = lambda i: jnp.where(i < 2 * items, i % items, items - 1)
    last = lambda i: jnp.maximum(i - 2 * items, 0)
    at_once = lambda value: (value, whole(value.shape))
    call = Call()
    call.arg(tok=(tokens.reshape(seqs, 1, length), pl.BlockSpec((pair, 1, length), lambda i: (late(i), 0, 0))), waves=at_once(saved.waves),
             small=(small, whole((feat, 128))), w_qkv=(w_qkv, ANYWHERE), w_out=at_once(w_out), start=(saved.start_o, lanes(feat, width, twice)),
             grad=(saved.grad, lanes(feat, width, twice)), project=(saved.project_o, lanes(3 * feat, width, soon)),
             powers=(saved.powers, pl.BlockSpec((pair, HEADS, length, length), lambda i: (soon(i), 0, 0, 0))), inv=at_once(saved.inv),
             mixed=at_once(saved.mixed_o), ln2=(saved.ln, ANYWHERE),
             middle_i=(saved.middle_o, ANYWHERE), act_i=(saved.act_o, ANYWHERE), down_i=(saved.down_o, ANYWHERE))
    call.out(d_in=((feat, n), F32, lanes(feat, width, late)), result=((feat, n), F32, lanes(feat, chunk, last)))
    vmem = lambda kind, *shape: pltpu.VMEM(shape, kind)
    call.temp(ln1=vmem(F32, 2, feat, 128), d_char=vmem(F32, feat, 128), low_f=vmem(BF16, feat, n), gp_f=vmem(BF16, 3 * feat, n),
              scores=vmem(F32, HEADS, length, length), grads=vmem(BF16, HEADS, length, length), grad_mixed=vmem(F32, feat, width),
              scaled=vmem(BF16, feat, width), lean=vmem(F32, seqs, HEADS, length), ga_f=vmem(BF16, feat, n), gs_f=vmem(F32, feat, 128),
              act=vmem(BF16, ff, n), middle=vmem(F32, feat, n), down_t=vmem(BF16, feat, ff), qkv=vmem(BF16, feat, 3 * feat),
              ln2_s=vmem(F32, 2, feat, 128), fetch_sems=pltpu.SemaphoreType.DMA((5,)))
    parts = 4
    if nz:
        devices = nz * 8
        per, down_per = feat // devices, ff // devices
        blocks = (nz,) + BLOCKS
        call.arg(d_down=(saved.d_down.reshape(blocks + (down_per, feat)), ANYWHERE))
        small_out = lambda *shape: (shape, F32, whole(shape))
        call.out(o_out=small_out(per, feat), o_down=small_out(down_per, feat), o_qkv=small_out(per, 3 * feat), o_time=small_out(per, feat),
                 o_char=small_out(per, chars), o_ln=small_out(4, per))
        call.temp(down_sums=Scatter.scratch(nz, (down_per, feat)), rest_sums=Scatter.scratch(nz, (per, 128 + feat)),
                  at_sums=Scatter.scratch(nz, (per, feat)) * parts, kept=vmem(BF16, nz, 2, 2, down_per, feat), kept_sem=pltpu.SemaphoreType.DMA,
                  d_at=[vmem(BF16, *blocks, per, feat)] * parts, d_rest=vmem(BF16, *blocks, per, 128 + feat))
    else:
        call.out(d_at=((feat, 4 * feat), BF16, whole((feat, 4 * feat))), d_rest=((feat, 128 + feat), BF16, whole((feat, 128 + feat))))

    def kernel(r):
        i = pl.program_id(0)
        fetch = [pltpu.make_async_copy(a, b, r.fetch_sems.at[k])
                 for k, (a, b) in enumerate(((r.w_qkv, r.qkv), (r.ln2, r.ln2_s), (r.middle_i, r.middle), (r.act_i, r.act), (r.down_i, r.down_t)))]
        if nz:
            c = place()[3]
            down = Scatter(nz, r.d_down, r.down_sums, r.kept)
            ats = [Scatter(nz, r.d_at[p], r.at_sums[5 * p:5 * p + 5]) for p in range(parts)]
            rest = Scatter(nz, r.d_rest, r.rest_sums)
            keep = pltpu.make_async_copy(r.d_down.at[pl.ds(0, nz), :, :, c], r.kept, r.kept_sem)

        def tall(value):
            value = value.astype(BF16)
            return value.reshape(blocks + (per, value.shape[-1])) if nz else value

        def prelude():
            if nz:
                greet(nz)
                keep.start()
            for copy in fetch:
                copy.start()
            r.ln1[...] = jnp.zeros_like(r.ln1)
            r.d_char[...] = jnp.zeros_like(r.d_char)
            r.gs_f[...] = jnp.zeros_like(r.gs_f)

        def products():
            pairs = [(r.mixed, r.ga_f)] + [(r.low_f, r.gp_f.at[pl.ds(p * feat, feat)]) for p in range(3)]
            for p, (left, right) in enumerate(pairs):
                product = tall(dot_nt(left[...], right[...]))
                if nz:
                    r.d_at[p][...] = product
                    ats[p].cores()
                    if p > 0:
                        ats[p - 1].corners()
                else:
                    r.d_at[:, p * feat:(p + 1) * feat] = product

        def rest_products():
            lane = lax.broadcasted_iota(jnp.int32, r.d_char.shape, 1)
            table = jnp.where(lane < chars, r.d_char[...], 0.0)
            for k, ref in enumerate((r.ln1.at[0], r.ln1.at[1], r.ln2_s.at[0], r.ln2_s.at[1])):
                table = jnp.where(lane == chars + k, jnp.sum(ref[...], axis=1, keepdims=True), table)
            r.d_rest[..., :128] = tall(table)
            r.d_rest[..., 128:] = tall(dot_nt(r.waves[...], r.gs_f[...].astype(BF16)))
            if nz:
                rest.cores()

        before = {}

        def at(step, *acts):
            before.setdefault(step, []).extend(acts)

        at(0, prelude)
        if nz:
            at(1, lambda: greeted(nz), down.cores, keep.wait)
            at(2, down.corners)
            at(items, down.sides)
        at(items, fetch[0].wait, fetch[1].wait, products)
        if nz:
            at(items + 1, ats[3].corners, ats[0].sides, ats[1].sides)
            at(items + 2, down.lines, ats[2].sides, ats[3].sides, ats[0].lines)
            at(items + 3, ats[1].lines)
        at(2 * items, rest_products, *[copy.wait for copy in fetch[2:]])
        if nz:
            at(2 * items, ats[2].lines, ats[3].lines)
            at(2 * items + 1, rest.corners)
            at(2 * items + 2, rest.sides)
        dispatch(i, before)

        @pl.when(i < items)
        def _():
            cols = pl.ds(pl.multiple_of(i * width, width), width)
            grad_low = r.grad[...].astype(BF16)
            r.ga_f[:, cols] = grad_low
            r.grad_mixed[...] = dot(r.w_out[...], grad_low).astype(BF16).astype(F32)
            for k in range(pair):
                here = pl.ds(k * length, length)
                item = i * pair + k
                there = pl.ds(pl.multiple_of(item * length, length), length)
                project, scaled, powers = r.project.at[:, here], r.scaled.at[:, here], r.powers.at[k]
                heads.scale_grad(r.grad_mixed.at[:, here], r.inv.at[item], r.mixed.at[:, there], scaled, r.lean.at[item])
                heads.grad_probs(project, scaled, r.scores)
                heads.grad_scores(powers, r.scores, r.lean.at[item], r.grads)
                heads.grad_project(project, scaled, powers, r.grads, r.gp_f, there)
            normed, _ = norm_rows(r.start[...])
            r.low_f[:, cols] = (normed * param(r.small, chars) + param(r.small, chars + 1)).astype(BF16)

        @pl.when((i >= items) & (i < 2 * items))
        def _():
            k = i - items
            cols = pl.ds(pl.multiple_of(k * width, width), width)
            grad_normed = dot(r.qkv[...], r.gp_f[:, cols])
            normed, inverse = norm_rows(r.start[...])
            d_in = r.grad[...] + norm_rows_back(grad_normed, param(r.small, chars), normed, inverse)
            r.d_in[...] = d_in
            r.ln1[0] += fold(grad_normed * normed)
            r.ln1[1] += fold(grad_normed)
            lane = lax.broadcasted_iota(jnp.int32, r.gs_f.shape, 1)
            sums = r.gs_f[...]
            for j in range(pair):
                part = d_in[:, j * length:(j + 1) * length]
                sums = jnp.where(lane == k * pair + j, jnp.sum(part, axis=1, keepdims=True), sums)
                one_hot = one_hot_of(r.tok[j])
                high = part.astype(BF16)
                rest_of = (part - high.astype(F32)).astype(BF16)
                r.d_char[...] += dot_nt(high, one_hot) + dot_nt(rest_of, one_hot)
            r.gs_f[...] = sums

        @pl.when(i >= 2 * items)
        def _():
            cols = pl.ds(pl.multiple_of((i - 2 * items) * chunk, chunk), chunk)
            r.result[...] = r.middle[:, cols] + dot(r.down_t[...], r.act[:, cols])

        if nz:
            @pl.when(i == 2 * items + chunks - 1)
            def _():
                rest.lines()
                r.o_down[...] = down.total()
                r.o_out[...] = ats[0].total()
                for p in range(3):
                    r.o_qkv[:, p * feat:(p + 1) * feat] = ats[1 + p].total()
                total = rest.total()
                r.o_time[...] = total[:, 128:]
                r.o_char[...] = total[:, :chars]
                r.o_ln[...] = total[:, :128].T[chars:chars + 4]

    return call.run(kernel, "backward", 2 * items + chunks, 1 if nz else None)


def hand_over(result, d_in, ln, *others, width=1024):
    feat, n = d_in.shape
    call = Call()
    turned = ((n, feat), F32, pl.BlockSpec((width, feat), lambda i: (i, 0)))
    call.arg(result=(result, lanes(feat, width)), d_in=(d_in, lanes(feat, width)), ln=(ln, whole(ln.shape)))
    call.arg(**{f"a{k}": (value, whole(value.shape)) for k, value in enumerate(others)})
    call.out(o_result=turned, o_d_in=turned, **{f"l{k}": ((1, ln.shape[1]), F32, whole((1, ln.shape[1]))) for k in range(4)})
    call.out(**{f"o{k}": (value.shape, F32, whole(value.shape)) for k, value in enumerate(others)})

    def kernel(r):
        r.o_result[...] = r.result[...].T
        r.o_d_in[...] = r.d_in[...].T

        @pl.when(pl.program_id(0) == 0)
        def _():
            for k, ref in enumerate((r.l0, r.l1, r.l2, r.l3)):
                ref[...] = r.ln[k:k + 1]
            for k in range(len(others)):
                getattr(r, f"o{k}")[...] = getattr(r, f"a{k}")[...]

    got = call.run(kernel, "hand_over", n // width)
    return got.o_result, got.o_d_in, [getattr(got, f"l{k}") for k in range(4)], [getattr(got, f"o{k}") for k in range(len(others))]


def make_body(gx, gy):
    def gathered(*shards):
        return [lax.all_gather(s, AXES, axis=0, tiled=True) for s in shards]

    def summed(part):
        return lax.psum_scatter(part.astype(F32), AXES, scatter_dimension=0, tiled=True)

    def body(tokens, timesteps, cotangent, char_table, time_weight, ln1_gain, ln1_bias, w_qkv, w_attn_out, ln2_gain, ln2_bias, w_up, w_down):
        feat = time_weight.shape[1]
        chars = char_table.shape[0]
        per = feat // (gx * gy)
        nz = gx // 2 if gy == 4 and gx % 8 == 0 and per % 16 == 0 else 0
        shards = [char_table.T, ln1_gain, ln1_bias, ln2_gain, ln2_bias, time_weight, w_qkv, w_attn_out, w_up, w_down]
        if not nz:
            shards = gathered(*shards)
        saved = forward(nz, tokens, timesteps, cotangent, *shards)
        if nz:
            small, w_qkv, w_out = (value.reshape(feat, value.shape[-1]) for value in (saved.first_o, saved.qkv_o, saved.out_o))
            got = backward(nz, chars, tokens, small, w_qkv, w_out, saved)
            ln, sums = got.o_ln, (got.o_char, got.o_time, got.o_qkv, got.o_out, saved.o_up, got.o_down)
        else:
            got = backward(nz, chars, tokens, saved.small, *shards[6:8], saved)
            up, down, at, rest = (summed(p) for p in (saved.d_up, saved.d_down, got.d_at, got.d_rest))
            ln, sums = rest[:, chars:chars + 4].T, (rest[:, :chars], rest[:, 128:], at[:, feat:], at[:, :feat], up, down)
        result, d_in, lns, (char, time, qkv, out, up, down) = hand_over(got.result, got.d_in, ln, *sums)
        g1, b1, g2, b2 = (value.reshape(per) for value in lns)
        return result, d_in, char.T, time, g1, b1, qkv, out, g2, b2, up, down
    return body


def solution(mesh):
    every = P(AXES)
    rows, cols = P(AXES, None), P(None, AXES)
    return jax.shard_map(
        make_body(mesh.shape[AXES[0]], mesh.shape[AXES[1]]),
        mesh=mesh,
        in_specs=(every, every, rows, cols, rows, every, every, rows, rows, every, every, rows, rows),
        out_specs=(rows, rows, cols, rows, every, every, rows, rows, every, every, rows, rows),
        check_vma=False,
    )
```

time: 1230 us -> 146 us (0.12)
  waiting for transfers between devices: 699 us -> 0 us
  blocking collectives: 200 us -> 0 us
  matrix products: 199 us -> 0 us
  Pallas kernels: 0 us -> 145 us
  local copies, waits for them, and re-layouts: 79.2 us -> 0 us
  other arithmetic: 30.9 us -> 0 us
  between operations: 14.9 us -> 0.82 us
    reduce_scatter x6 -> x0, waiting for transfers between devices: 697 us -> none  [the longest x1 143 us: body(): lax.psum_scatter(ffn_grads[2], ('gx', 'gy'), scatter_dimension=0, tiled=T...]
    dot_general x23 -> x0, matrix products: 199 us -> none  [the longest x1 44.2 us: ffn_parts(): hidden = jnp.dot(normed_low, up_weight, preferred_element_type=jnp.float32)]
    pallas_call x0 -> x3, Pallas kernels: none -> 145 us  [run(): pl.pallas_call(body, grid=(steps,), in_specs=[spec for _, spec in self.in...]
    all_gather x3 -> x0, blocking collectives: 126 us -> none  [the longest x1 45 us: body(): lax.all_gather(time_weight, ('gx', 'gy'), axis=0, tiled=True)]
    unnamed x2 -> x0, blocking collectives: 74.4 us -> none
    unnamed x102 -> x0, local copies, waits for them, and re-layouts: 34.5 us -> none
    reshape x3 -> x0, local copies, waits for them, and re-layouts: 25.1 us -> none  [the longest x1 16.3 us: attention_parts(): project.reshape(seq_count, start.shape[0] // seq_count, 3, HEADS, head_size)]
    convert_element_type x6 -> x0, other arithmetic: 13.1 us -> none  [the longest x1 12.4 us: attention_backward(): grad_scores = (probabilities * (grad_probs - jnp.sum(grad_probs * probabi...]
  transfers between devices with their start and end apart: 9 -> 0, of which waited for: 6 -> 0; matrix products, arithmetic and copies ran while one was open for 16% -> 0% of each run, Pallas kernels for 0% -> 0%
where the time goes in v3:
time: 146 us
  Pallas kernels  145 us (99%)
    pallas_call x3, Pallas kernels, run(): pl.pallas_call(body, grid=(steps,), in_specs=[spec for _, spec in self.in...  145 us

profile of v3, /device:TPU:0, one launch (start us, length us, event | category | flops | bytes accessed | tf_op | source)
XLA Modules:
  0.0 145.9 jit_solution(3616400280089274089)
XLA Ops:
  0.6 87.6 %forward_and_ffn.1 = (f32[512,2048]{1,0:T(8,128)}, bf16[512,2048]{1,0:T(8,128)(2,1)}, bf16[1536,2048]{1,0:T(8,128)(2,1)}, bf16[8,8,256,256]{3,2,1,0:T(8,128)(2,1...) custom-call(s32[8,1,256]{2,1,0:T(1,128)} %bitcast.20, ...), custom_call_target="tpu_custom_call" | custom-call | tf_op jit(solution)/shard_map/forward_and_ffn/pallas_call | solution.py:233
  88.3 50.4 %backward.1 = (f32[512,2048]{1,0:T(8,128)}, f32[512,2048]{1,0:T(8,128)}, f32[16,512]{1,0:T(8,128)}, f32[64,512]{1,0:T(8,128)}, f32[16,1536]{1,0:T(8,128)}, /*ind...) custom-call(s32[8,1,256]{2,1,0:T(1,128)} %bitcast.21, bf16[512,128]{1,0:T(8,128)(2,1)} %get-tuple-element.48.refs_1_, ...), custom_call_target="tpu_custom_call" | custom-call | tf_op jit(solution)/shard_map/backward/pallas_call | solution.py:233
  138.8 7.0 %hand_over.1 = (f32[2048,512]{1,0:T(8,128)}, f32[2048,512]{1,0:T(8,128)}, f32[1,16]{1,0:T(1,128)}, f32[1,16]{1,0:T(1,128)}, f32[1,16]{1,0:T(1,128)}, /*index=5*/...) custom-call(f32[512,2048]{1,0:T(8,128)} %get-tuple-element.63.refs_0, ...), custom_call_target="tpu_custom_call" | custom-call | tf_op jit(solution)/shard_map/hand_over/pallas_call | solution.py:233
